TPU v7x, 32 devices: a whole 2x2x4 slice. The times are simulated.
32 devices in a mesh: seq: 2 (over core), fsdp: 16 (over z, y, x).
Axes of the slice: x: 2, y: 2, z: 4, core: 2. Of those that a mesh axis runs over, the one named last changes fastest.
Arguments:
- tokens: bfloat16 [64, 492, 768], P('fsdp', 'seq'), may hold values from -8 to 8
- read_memory: bfloat16 [64, 10, 768], P('fsdp'), may hold values from -6 to 6
- valid_count: int32 [64], P('fsdp'), may hold values from 123 to 492, as said below
- cotangent: bfloat16 [64, 512, 768], P('fsdp', 'seq'), may hold values from -6 to 6
- query_weight: bfloat16 [768, 768], P(('seq', 'fsdp')), may hold values from -0.3125 to 0.3125
- query_bias: bfloat16 [768], P(('seq', 'fsdp')), may hold values from -1.75 to 1.75
- key_weight: bfloat16 [768, 768], P(('seq', 'fsdp')), may hold values from -0.3125 to 0.3125
- value_weight: bfloat16 [768, 768], P(('seq', 'fsdp')), may hold values from -0.21875 to 0.21875
- value_bias: bfloat16 [768], P(('seq', 'fsdp')), may hold values from -1.75 to 1.75
- output_weight: bfloat16 [768, 768], P(('seq', 'fsdp')), may hold values from -0.875 to 0.875
- output_bias: bfloat16 [768], P(('seq', 'fsdp')), may hold values from -1.75 to 1.75
- first_gain: bfloat16 [768], P(('seq', 'fsdp')), may hold values from 0.5 to 1.5
- first_shift: bfloat16 [768], P(('seq', 'fsdp')), may hold values from -1.75 to 1.75
- inner_weight: bfloat16 [768, 3072], P(('seq', 'fsdp')), may hold values from -0.21875 to 0.21875
- inner_bias: bfloat16 [3072], P(('seq', 'fsdp')), may hold values from -1.75 to 1.75
- outer_weight: bfloat16 [3072, 768], P(('seq', 'fsdp')), may hold values from -0.109375 to 0.109375
- outer_bias: bfloat16 [768], P(('seq', 'fsdp')), may hold values from -1.75 to 1.75
- second_gain: bfloat16 [768], P(('seq', 'fsdp')), may hold values from 0.5 to 1.5
- second_shift: bfloat16 [768], P(('seq', 'fsdp')), may hold values from -1.75 to 1.75
Outputs:
- layer_out: bfloat16 [64, 512, 768], P('fsdp', 'seq')
- tokens_grad: bfloat16 [64, 492, 768], P('fsdp', 'seq')
- memory_grad: float32 [64, 10, 768], P('fsdp')
- query_weight_grad: float32 [768, 768], P(('seq', 'fsdp'))
- query_bias_grad: float32 [768], P(('seq', 'fsdp'))
- key_weight_grad: float32 [768, 768], P(('seq', 'fsdp'))
- value_weight_grad: float32 [768, 768], P(('seq', 'fsdp'))
- value_bias_grad: float32 [768], P(('seq', 'fsdp'))
- output_weight_grad: float32 [768, 768], P(('seq', 'fsdp'))
- output_bias_grad: float32 [768], P(('seq', 'fsdp'))
- first_gain_grad: float32 [768], P(('seq', 'fsdp'))
- first_shift_grad: float32 [768], P(('seq', 'fsdp'))
- inner_weight_grad: float32 [768, 3072], P(('seq', 'fsdp'))
- inner_bias_grad: float32 [3072], P(('seq', 'fsdp'))
- outer_weight_grad: float32 [3072, 768], P(('seq', 'fsdp'))
- outer_bias_grad: float32 [768], P(('seq', 'fsdp'))
- second_gain_grad: float32 [768], P(('seq', 'fsdp'))
- second_shift_grad: float32 [768], P(('seq', 'fsdp'))
Inputs may be any that keep to these rules, and one draw needn't show every extreme that they name: `valid_count`: real tokens of a segment; the first of every 4 segments is full.
All inputs are finite; a program needn't handle non-finite values.
Results may differ from a plain program's by a relative error of at most 0.015.
The roundings to bfloat16 on the way count: a program that leaves them out, or rounds other values in their place, can miss the bound.
Values may be sent and summed in bfloat16 or wider, within the bound.
No kernel may reach another device: no remote copies, remote signals or barrier semaphores. Data moves between devices by JAX's collectives and lax.ppermute only.
A program may use at most 192 MiB of HBM per device.

v0:
```python
import math

import jax
import jax.numpy as jnp
from jax import lax
from jax.sharding import PartitionSpec as P

HD = 64
MEM = 10
MB = 2
SEG = 512


EPSILON = 1e-12
ROOT_HALF = math.sqrt(0.5)
INV_ROOT_TAU = 1.0 / math.sqrt(2.0 * math.pi)


def normalize(resid):
    centre = resid - jnp.mean(resid, axis=-1, keepdims=True)
    inverse = lax.rsqrt(jnp.mean(centre * centre, axis=-1, keepdims=True) + EPSILON)
    return (centre * inverse, inverse)


def norm_back(grad_out, normed, inverse, gain):
    scaled = grad_out * gain
    return inverse * (
        scaled
        - jnp.mean(scaled, axis=-1, keepdims=True)
        - normed * jnp.mean(scaled * normed, axis=-1, keepdims=True)
    )


def gelu_slope(inner):
    return (
        0.5 * (1.0 + lax.erf(inner * ROOT_HALF))
        + inner * jnp.exp(-0.5 * inner * inner) * INV_ROOT_TAU
    )


def key_keep(valid):
    places = jnp.arange(SEG)
    return (places < MEM) | (places >= SEG - MEM) | (places - MEM < valid)


def head_split(block):
    return block.reshape(block.shape[0], -1, HD)


def segment_scores(stacked, valid):
    query_h = head_split(stacked[0])
    keys_h = head_split(stacked[1])
    scores = jnp.einsum(
        "qhe,khe->hqk", query_h, keys_h, preferred_element_type=jnp.float32
    ) * HD ** (-0.5)
    keep = key_keep(valid)
    return (
        jnp.where(keep[None, None, :], scores, -1000000000.0),
        query_h,
        keys_h,
        head_split(stacked[2]),
    )


def attend_segment(inputs):
    stacked, valid = inputs
    scores, query_h, keys_h, values_h = segment_scores(stacked, valid)
    top = jnp.max(scores, axis=-1, keepdims=True)
    weights = jnp.exp(scores - top)
    total = jnp.sum(weights, axis=-1, keepdims=True)
    probs = weights / total
    mixed = jnp.einsum(
        "hqk,khe->qhe", probs.astype(jnp.bfloat16), values_h, preferred_element_type=jnp.float32
    )
    return (mixed.reshape(SEG, -1).astype(jnp.bfloat16), (top + jnp.log(total))[..., 0])


def attend_back(inputs):
    stacked, grad_mixed, log_total, valid = inputs
    scores, query_h, keys_h, values_h = segment_scores(stacked, valid)
    probs = jnp.exp(scores - log_total[..., None])
    grad_h = head_split(grad_mixed)
    grad_probs = jnp.einsum("qhe,khe->hqk", grad_h, values_h, preferred_element_type=jnp.float32)
    delta = jnp.sum(probs * grad_probs, axis=-1, keepdims=True)
    grad_scores = (probs * (grad_probs - delta)).astype(jnp.bfloat16)
    scale = HD ** (-0.5)
    grad_query = (
        jnp.einsum("hqk,khe->qhe", grad_scores, keys_h, preferred_element_type=jnp.float32) * scale
    )
    grad_keys = (
        jnp.einsum("hqk,qhe->khe", grad_scores, query_h, preferred_element_type=jnp.float32) * scale
    )
    grad_values = jnp.einsum(
        "hqk,qhe->khe", probs.astype(jnp.bfloat16), grad_h, preferred_element_type=jnp.float32
    )
    return jnp.stack(
        [grad_query.reshape(SEG, -1), grad_keys.reshape(SEG, -1), grad_values.reshape(SEG, -1)]
    ).astype(jnp.bfloat16)


def column_sum(values):
    return jnp.sum(values.astype(jnp.float32), axis=0)


def micro_pass(gathered, tokens_part, memory_part, valid_part, cot_part, side):
    (
        query_weight,
        query_bias,
        key_weight,
        value_weight,
        value_bias,
        output_weight,
        output_bias,
        first_gain,
        first_shift,
        inner_weight,
        inner_bias,
        outer_weight,
        outer_bias,
        second_gain,
        second_shift,
    ) = gathered
    count = tokens_part.shape[0]
    rows = jnp.where(
        side == 0,
        jnp.concatenate([memory_part, tokens_part], axis=1),
        jnp.concatenate([tokens_part, memory_part], axis=1),
    )
    local_rows = rows.shape[1]
    width = rows.shape[2]
    flat = rows.reshape(-1, width)
    query = (
        jnp.dot(flat, query_weight, preferred_element_type=jnp.float32)
        + query_bias.astype(jnp.float32)
    ).astype(jnp.bfloat16)
    keys = jnp.dot(flat, key_weight, preferred_element_type=jnp.float32).astype(jnp.bfloat16)
    values = (
        jnp.dot(flat, value_weight, preferred_element_type=jnp.float32)
        + value_bias.astype(jnp.float32)
    ).astype(jnp.bfloat16)
    stacked = jnp.stack(
        [
            query.reshape(count, local_rows, width),
            keys.reshape(count, local_rows, width),
            values.reshape(count, local_rows, width),
        ],
        axis=1,
    )
    heads = lax.all_to_all(stacked, "seq", split_axis=3, concat_axis=2, tiled=True)
    mixed, log_total = lax.map(attend_segment, (heads, valid_part))
    attended = lax.all_to_all(mixed, "seq", split_axis=1, concat_axis=2, tiled=True).reshape(
        -1, width
    )
    branch = jnp.dot(
        attended, output_weight, preferred_element_type=jnp.float32
    ) + output_bias.astype(jnp.float32)
    normed_one, inverse_one = normalize(flat.astype(jnp.float32) + branch)
    first = normed_one * first_gain.astype(jnp.float32) + first_shift.astype(jnp.float32)
    first_low = first.astype(jnp.bfloat16)
    inner = jnp.dot(
        first_low, inner_weight, preferred_element_type=jnp.float32
    ) + inner_bias.astype(jnp.float32)
    active = jax.nn.gelu(inner, approximate=False).astype(jnp.bfloat16)
    outer = jnp.dot(active, outer_weight, preferred_element_type=jnp.float32) + outer_bias.astype(
        jnp.float32
    )
    normed_two, inverse_two = normalize(first + outer)
    result = (
        normed_two * second_gain.astype(jnp.float32) + second_shift.astype(jnp.float32)
    ).astype(jnp.bfloat16)
    result = result.reshape(count, local_rows, width)
    grad_out = cot_part.reshape(-1, width).astype(jnp.float32)
    grad_gain_two = jnp.sum(grad_out * normed_two, axis=0)
    grad_shift_two = jnp.sum(grad_out, axis=0)
    grad_res_two = norm_back(grad_out, normed_two, inverse_two, second_gain.astype(jnp.float32))
    grad_outer = grad_res_two.astype(jnp.bfloat16)
    grad_outer_bias = column_sum(grad_outer)
    grad_outer_weight = jnp.einsum(
        "rf,rd->fd", active, grad_outer, preferred_element_type=jnp.float32
    )
    grad_active = jnp.einsum(
        "rd,fd->rf", grad_outer, outer_weight, preferred_element_type=jnp.float32
    )
    grad_inner = (grad_active * gelu_slope(inner)).astype(jnp.bfloat16)
    grad_inner_bias = column_sum(grad_inner)
    grad_inner_weight = jnp.einsum(
        "rd,rf->df", first_low, grad_inner, preferred_element_type=jnp.float32
    )
    grad_first = grad_res_two + jnp.einsum(
        "rf,df->rd", grad_inner, inner_weight, preferred_element_type=jnp.float32
    )
    grad_gain_one = jnp.sum(grad_first * normed_one, axis=0)
    grad_shift_one = jnp.sum(grad_first, axis=0)
    grad_res_one = norm_back(grad_first, normed_one, inverse_one, first_gain.astype(jnp.float32))
    grad_branch = grad_res_one.astype(jnp.bfloat16)
    grad_output_bias = column_sum(grad_branch)
    grad_output_weight = jnp.einsum(
        "re,rd->ed", attended, grad_branch, preferred_element_type=jnp.float32
    )
    grad_attended = jnp.einsum(
        "rd,ed->re", grad_branch, output_weight, preferred_element_type=jnp.float32
    ).astype(jnp.bfloat16)
    grad_mixed = lax.all_to_all(
        grad_attended.reshape(count, local_rows, width),
        "seq",
        split_axis=2,
        concat_axis=1,
        tiled=True,
    )
    grad_stacked = lax.map(attend_back, (heads, grad_mixed, log_total, valid_part))
    grad_local = lax.all_to_all(grad_stacked, "seq", split_axis=2, concat_axis=3, tiled=True)
    grad_query = grad_local[:, 0].reshape(-1, width)
    grad_keys = grad_local[:, 1].reshape(-1, width)
    grad_values = grad_local[:, 2].reshape(-1, width)
    grad_query_weight = jnp.einsum(
        "rd,re->de", flat, grad_query, preferred_element_type=jnp.float32
    )
    grad_query_bias = column_sum(grad_query)
    grad_key_weight = jnp.einsum("rd,re->de", flat, grad_keys, preferred_element_type=jnp.float32)
    grad_value_weight = jnp.einsum(
        "rd,re->de", flat, grad_values, preferred_element_type=jnp.float32
    )
    grad_value_bias = column_sum(grad_values)
    grad_rows = (
        grad_res_one
        + jnp.einsum("re,de->rd", grad_query, query_weight, preferred_element_type=jnp.float32)
        + jnp.einsum("re,de->rd", grad_keys, key_weight, preferred_element_type=jnp.float32)
        + jnp.einsum("re,de->rd", grad_values, value_weight, preferred_element_type=jnp.float32)
    )
    grad_rows = grad_rows.reshape(count, local_rows, width)
    memory_rows = memory_part.shape[1]
    token_rows = tokens_part.shape[1]
    grad_tokens = jnp.where(side == 0, grad_rows[:, memory_rows:], grad_rows[:, :token_rows])
    grad_memory = jnp.where(side == 0, grad_rows[:, :memory_rows], grad_rows[:, token_rows:])
    local_grads = (
        grad_query_weight,
        grad_query_bias,
        grad_key_weight,
        grad_value_weight,
        grad_value_bias,
        grad_output_weight,
        grad_output_bias,
        grad_gain_one,
        grad_shift_one,
        grad_inner_weight,
        grad_inner_bias,
        grad_outer_weight,
        grad_outer_bias,
        grad_gain_two,
        grad_shift_two,
    )
    return (result, grad_tokens, grad_memory, local_grads)


def per_device(
    tokens,
    read_memory,
    valid_count,
    cotangent,
    query_weight,
    query_bias,
    key_weight,
    value_weight,
    value_bias,
    output_weight,
    output_bias,
    first_gain,
    first_shift,
    inner_weight,
    inner_bias,
    outer_weight,
    outer_bias,
    second_gain,
    second_shift,
):
    side = lax.axis_index("seq")
    count = tokens.shape[0] // MB
    results = []
    token_grads = []
    memory_grads = []
    totals = ()
    for micro_index in range(MB):
        gathered = (
            lax.all_gather(query_weight, ("seq", "fsdp"), axis=0, tiled=True),
            lax.all_gather(query_bias, ("seq", "fsdp"), axis=0, tiled=True),
            lax.all_gather(key_weight, ("seq", "fsdp"), axis=0, tiled=True),
            lax.all_gather(value_weight, ("seq", "fsdp"), axis=0, tiled=True),
            lax.all_gather(value_bias, ("seq", "fsdp"), axis=0, tiled=True),
            lax.all_gather(output_weight, ("seq", "fsdp"), axis=0, tiled=True),
            lax.all_gather(output_bias, ("seq", "fsdp"), axis=0, tiled=True),
            lax.all_gather(first_gain, ("seq", "fsdp"), axis=0, tiled=True),
            lax.all_gather(first_shift, ("seq", "fsdp"), axis=0, tiled=True),
            lax.all_gather(inner_weight, ("seq", "fsdp"), axis=0, tiled=True),
            lax.all_gather(inner_bias, ("seq", "fsdp"), axis=0, tiled=True),
            lax.all_gather(outer_weight, ("seq", "fsdp"), axis=0, tiled=True),
            lax.all_gather(outer_bias, ("seq", "fsdp"), axis=0, tiled=True),
            lax.all_gather(second_gain, ("seq", "fsdp"), axis=0, tiled=True),
            lax.all_gather(second_shift, ("seq", "fsdp"), axis=0, tiled=True),
        )
        start = micro_index * count
        tok_block = tokens[start : start + count]
        mem_block = read_memory[start : start + count]
        valid_block = valid_count[start : start + count]
        cot_block = cotangent[start : start + count]
        result, grad_tokens, grad_memory, local_grads = micro_pass(
            gathered, tok_block, mem_block, valid_block, cot_block, side
        )
        results.append(result)
        token_grads.append(grad_tokens.astype(jnp.bfloat16))
        memory_grads.append(grad_memory)
        (
            grad_qweight,
            grad_qbias,
            grad_kweight,
            grad_vweight,
            grad_vbias,
            grad_oweight,
            grad_obias,
            grad_gone,
            grad_sone,
            grad_iweight,
            grad_ibias,
            grad_uweight,
            grad_ubias,
            grad_gtwo,
            grad_stwo,
        ) = local_grads
        local_grads = (
            lax.psum_scatter(grad_qweight, ("seq", "fsdp"), scatter_dimension=0, tiled=True),
            lax.psum_scatter(grad_qbias, ("seq", "fsdp"), scatter_dimension=0, tiled=True),
            lax.psum_scatter(grad_kweight, ("seq", "fsdp"), scatter_dimension=0, tiled=True),
            lax.psum_scatter(grad_vweight, ("seq", "fsdp"), scatter_dimension=0, tiled=True),
            lax.psum_scatter(grad_vbias, ("seq", "fsdp"), scatter_dimension=0, tiled=True),
            lax.psum_scatter(grad_oweight, ("seq", "fsdp"), scatter_dimension=0, tiled=True),
            lax.psum_scatter(grad_obias, ("seq", "fsdp"), scatter_dimension=0, tiled=True),
            lax.psum_scatter(grad_gone, ("seq", "fsdp"), scatter_dimension=0, tiled=True),
            lax.psum_scatter(grad_sone, ("seq", "fsdp"), scatter_dimension=0, tiled=True),
            lax.psum_scatter(grad_iweight, ("seq", "fsdp"), scatter_dimension=0, tiled=True),
            lax.psum_scatter(grad_ibias, ("seq", "fsdp"), scatter_dimension=0, tiled=True),
            lax.psum_scatter(grad_uweight, ("seq", "fsdp"), scatter_dimension=0, tiled=True),
            lax.psum_scatter(grad_ubias, ("seq", "fsdp"), scatter_dimension=0, tiled=True),
            lax.psum_scatter(grad_gtwo, ("seq", "fsdp"), scatter_dimension=0, tiled=True),
            lax.psum_scatter(grad_stwo, ("seq", "fsdp"), scatter_dimension=0, tiled=True),
        )
        if micro_index == 0:
            totals = tuple(local_grads)
        else:
            totals = tuple((total + grad for total, grad in zip(totals, local_grads)))
    memory_total = lax.psum(
        jnp.concatenate(memory_grads, axis=0).astype(jnp.bfloat16), "seq"
    ).astype(jnp.float32)
    layer_out = jnp.concatenate(results, axis=0)
    tokens_grad = jnp.concatenate(token_grads, axis=0)
    return (
        layer_out,
        tokens_grad,
        memory_total,
        totals[0],
        totals[1],
        totals[2],
        totals[3],
        totals[4],
        totals[5],
        totals[6],
        totals[7],
        totals[8],
        totals[9],
        totals[10],
        totals[11],
        totals[12],
        totals[13],
        totals[14],
    )


def solution(mesh):
    return jax.shard_map(
        per_device,
        mesh=mesh,
        in_specs=(
            P("fsdp", "seq", None),
            P("fsdp", None, None),
            P("fsdp"),
            P("fsdp", "seq", None),
            P(("seq", "fsdp"), None),
            P(("seq", "fsdp")),
            P(("seq", "fsdp"), None),
            P(("seq", "fsdp"), None),
            P(("seq", "fsdp")),
            P(("seq", "fsdp"), None),
            P(("seq", "fsdp")),
            P(("seq", "fsdp")),
            P(("seq", "fsdp")),
            P(("seq", "fsdp"), None),
            P(("seq", "fsdp")),
            P(("seq", "fsdp"), None),
            P(("seq", "fsdp")),
            P(("seq", "fsdp")),
            P(("seq", "fsdp")),
        ),
        out_specs=(
            P("fsdp", "seq", None),
            P("fsdp", "seq", None),
            P("fsdp", None, None),
            P(("seq", "fsdp"), None),
            P(("seq", "fsdp")),
            P(("seq", "fsdp"), None),
            P(("seq", "fsdp"), None),
            P(("seq", "fsdp")),
            P(("seq", "fsdp"), None),
            P(("seq", "fsdp")),
            P(("seq", "fsdp")),
            P(("seq", "fsdp")),
            P(("seq", "fsdp"), None),
            P(("seq", "fsdp")),
            P(("seq", "fsdp"), None),
            P(("seq", "fsdp")),
            P(("seq", "fsdp")),
            P(("seq", "fsdp")),
        ),
        check_vma=False,
    )
```

profile of v0, /device:TPU:0, one launch (start us, length us, event | category | flops | bytes accessed | tf_op | source)
XLA Modules:
  0.0 1120.9 jit_solution(3839700772748361167)
XLA Ops:
  18.8 42.5 %all-reduce.19 = (bf16[768]{0:T(1024)(128)(2,1)S(1)}, bf16[768]{0:T(1024)(128)(2,1)S(1)}, bf16[768]{0:T(1024)(128)(2,1)S(1)}, bf16[768]{0:T(1024)(128)(2,1)S(1)}...) all-reduce(bf16[768]{0:T(1024)(128)(2,1)S(1)} %dynamic-update-slice, ...), channel_id=1, replica_groups=mesh['seq'=2,'fsdp'=16] {'seq','fsdp'}, use_global_device_ids=true, to_apply=%add.1 | all-reduce | flops 9216 | bytes 36864
  61.2 3.3 fusion.115
  64.6 3.5 broadcast_select_fusion
  77.4 46.6 %all-gather.11.cloned.1.call-done = bf16[768,768]{1,0:T(8,128)(2,1)} async-done(((bf16[24,768]{1,0:T(8,128)(2,1)}), bf16[768,768]{1,0:T(8,128)(2,1)}) %all-gather.11.cloned.1.call-update) | async-done | bytes 1179664 | tf_op jit(solution)/shard_map/all_gather | solution.py:287
  126.7 53.2 %all-gather.9.cloned.1.call-done = bf16[768,768]{1,0:T(8,128)(2,1)} async-done(((bf16[24,768]{1,0:T(8,128)(2,1)}), bf16[768,768]{1,0:T(8,128)(2,1)}) %all-gather.9.cloned.1.call-update) | async-done | bytes 1179664 | tf_op jit(solution)/shard_map/all_gather | solution.py:286
  179.9 2.9 convolution_convert_fusion.3
  182.9 2.3 copy.173
  185.2 3.4 pad_maximum_fusion
  188.6 5.8 all_to_all.138
  194.4 3.8 copy.175
  198.2 5.3 all_to_all.103
  204.5 13.6 %while.52 = (s32[]{:T(128)}, bf16[2,512,384]{1,2,0:T(8,128)(2,1)}, f32[2,6,512]{2,1,0:T(8,128)S(1)}, bf16[2,3,512,384]{2,3,1,0:T(8,128)(2,1)S(1)}, s32[2]{0:T(128)S(1)}, /*index=5*/s32[]{:T(128)}, s32[]{:T(128)}, s32[]{}, s32[]{}) while((s32[]{:T(128)}, bf16[2,512,384]{1,2,0:T(8,128)(2,1)}, f32[2,6,512]{2,1,0:T(8,128)S(1)}, ...), condition=%wide.region_3.4_spmd, body=%wide.region_0.3_spmd.sunk | while | flops 421724160 | bytes 23706260 | solution.py:150
  218.1 3.3 copy.176
  221.4 5.5 all_to_all.139
  227.8 7.9 all-gather.13.cloned.1.call-done
  235.7 3.3 fusion.122
  240.8 2.3 copy.179
  244.7 2.3 copy.181
  247.1 2.9 convolution_convert_fusion.2
  250.0 3.0 copy.180
  253.0 4.8 pad_maximum_fusion.1
  257.8 6.0 all_to_all.140
  263.8 3.8 copy.182
  267.6 5.3 all_to_all.110
  273.9 13.6 %while.53 = (s32[]{:T(128)}, bf16[2,512,384]{1,2,0:T(8,128)(2,1)}, f32[2,6,512]{2,1,0:T(8,128)S(1)}, bf16[2,3,512,384]{2,3,1,0:T(8,128)(2,1)S(1)}, s32[2]{0:T(128)S(1)}, /*index=5*/s32[]{:T(128)}, s32[]{:T(128)}, s32[]{}, s32[]{}) while((s32[]{:T(128)}, bf16[2,512,384]{1,2,0:T(8,128)(2,1)}, f32[2,6,512]{2,1,0:T(8,128)S(1)}, ...), condition=%wide.region_11.12_spmd, body=%wide.region_8.11_spmd.sunk | while | flops 421724160 | bytes 23706260 | solution.py:150
  287.6 3.3 copy.183
  290.9 5.8 all_to_all.141
  301.1 4.8 fusion.105
  305.9 2.7 copy-done.96
  308.6 31.4 %fusion.44 = (bf16[512,3072]{1,0:T(8,128)(2,1)}, bf16[512,3072]{1,0:T(8,128)(2,1)}, f32[512,3072]{1,0:T(8,128)}) fusion(f32[3072]{0:T(1024)S(1)} %copy-done.69, f32[512,3072]{1,0:T(8,128)S(1)} %fusion.105, bf16[768,3072]{1,0:T(8,128)(2,1)S(1)} %copy-done.89, f32[512,768]{1,0:T(8,128)S(1)} %copy-done.44, f32[768]{0:T(1024)S(1)} %copy-done.52, ...), kind=kOutput, calls=%fused_computation.92 | convolution fusion | flops 2625503232 | bytes 25188352 | tf_op jit(solution)/shard_map/dot_general | solution.py:160
  340.0 26.2 %all-gather.17.cloned.1.call-done = bf16[3072,768]{1,0:T(8,128)(2,1)} async-done(((bf16[96,768]{1,0:T(8,128)(2,1)}), bf16[3072,768]{1,0:T(8,128)(2,1)}) %all-gather.17.cloned.1.call-update) | async-done | bytes 4718608 | tf_op jit(solution)/shard_map/all_gather | solution.py:295
  366.3 6.2 fusion.125
  372.8 2.8 fusion.124
  378.8 3.0 convert_reduce_fusion.4
  381.8 5.3 convert_reduce_fusion.1
  387.1 3.6 multiply_reduce_fusion.3
  390.7 7.2 convert_reduce_fusion
  398.0 3.8 convert_reduce_fusion.7
  405.0 2.3 convolution_add_fusion.2
  410.0 4.4 all_to_all.142
  416.1 2.6 all_to_all.117
  420.4 22.4 %while.54 = (s32[]{:T(128)}, bf16[2,3,512,384]{2,3,1,0:T(8,128)(2,1)}, bf16[2,3,512,384]{2,3,1,0:T(8,128)(2,1)S(1)}, s32[2]{0:T(128)S(1)}, f32[2,6,512]{2,1,0:T(...) while((s32[]{:T(128)}, bf16[2,3,512,384]{2,3,1,0:T(8,128)(2,1)}, ...), condition=%wide.region_22.23_spmd, body=%wide.region_20.22_spmd.sunk | while | flops 1034747904 | bytes 56711840 | solution.py:210
  442.9 7.0 copy.187
  451.4 4.4 all_to_all.143
  455.8 4.9 all-to-all-start.5
  462.4 3.0 all_to_all.125
  467.1 22.5 %while.55 = (s32[]{:T(128)}, bf16[2,3,512,384]{2,3,1,0:T(8,128)(2,1)}, bf16[2,3,512,384]{2,3,1,0:T(8,128)(2,1)S(1)}, s32[2]{0:T(128)S(1)}, f32[2,6,512]{2,1,0:T(...) while((s32[]{:T(128)}, bf16[2,3,512,384]{2,3,1,0:T(8,128)(2,1)}, ...), condition=%wide.region_29.30_spmd, body=%wide.region_27.29_spmd.sunk | while | flops 1034747904 | bytes 56711840 | solution.py:210
  489.5 3.4 copy.188
  492.9 2.8 copy.189
  498.9 6.5 copy.197
  505.4 5.8 all_to_all.144
  512.9 2.8 copy.199
  540.1 5.3 fusion.101
  545.4 5.3 convolution_add_fusion
  551.4 5.5 fusion.107
  556.9 5.7 convolution_add_fusion.1
  566.5 40.6 %all-reduce.18 = (f32[768]{0:T(1024)S(1)}, f32[768]{0:T(1024)S(1)}, f32[768]{0:T(1024)S(1)}, f32[768]{0:T(1024)S(1)}, f32[768]{0:T(1024)S(1)}, /*index=5*/f32[30...) all-reduce(f32[768]{0:T(1024)S(1)} %add.434, ...), channel_id=18, replica_groups=mesh['seq'=2,'fsdp'=16] {'seq','fsdp'}, use_global_device_ids=true, to_apply=%region_34.35.clone | all-reduce | flops 9216 | bytes 73728
  611.7 2.3 fusion.128
  621.4 3.8 psum.7
  629.1 2.7 pad_maximum_fusion.3
  633.0 93.0 %reduce-scatter.9.cloned.1.call-done = f32[24,768]{1,0:T(8,128)} async-done(((f32[768,768]{1,0:T(8,128)}), f32[24,768]{1,0:T(8,128)}) %reduce-scatter.9.cloned.1.call-update) | async-done | bytes 73744 | tf_op jit(solution)/shard_map/reduce_scatter | solution.py:331
  726.0 104.6 %reduce-scatter.7.cloned.1.call-done = f32[24,768]{1,0:T(8,128)} async-done(((f32[768,768]{1,0:T(8,128)}), f32[24,768]{1,0:T(8,128)}) %reduce-scatter.7.cloned.1.call-update) | async-done | bytes 73744 | tf_op jit(solution)/shard_map/reduce_scatter | solution.py:329
  830.6 141.1 %reduce-scatter.17.cloned.1.call-done = f32[96,768]{1,0:T(8,128)} async-done(((f32[3072,768]{1,0:T(8,128)}), f32[96,768]{1,0:T(8,128)}) %reduce-scatter.17.cloned.1.call-update) | async-done | bytes 294928 | tf_op jit(solution)/shard_map/reduce_scatter | solution.py:340
  971.7 141.9 %reduce-scatter.15.cloned.1.call-done = f32[24,3072]{1,0:T(8,128)} async-done(((f32[768,3072]{1,0:T(8,128)}), f32[24,3072]{1,0:T(8,128)}) %reduce-scatter.15.cloned.1.call-update) | async-done | bytes 294928 | tf_op jit(solution)/shard_map/reduce_scatter | solution.py:338
  (444 shorter events, 173.4 us)
Async XLA Ops:
  7.2 57.3 %copy-start.56 = (bf16[4,10,768]{2,0,1:T(4,128)(2,1)S(1)}, bf16[4,10,768]{2,0,1:T(4,128)(2,1)}, u32[]{:S(2)}) copy-start(bf16[4,10,768]{2,0,1:T(4,128)(2,1)} %param.28) | copy-start | bytes 184324
  7.2 67.5 %all-gather.7.cloned.1.call-start = ((), (), s32[]{:S(2)}) async-start(), calls=%async_computation.14 | async-start | bytes 1216512 | tf_op jit(solution)/shard_map/all_gather | solution.py:284
  7.9 116.1 %all-gather.11.cloned.1.call-start = ((), (), s32[]{:S(2)}) async-start(), calls=%async_computation.16 | async-start | bytes 1216512 | tf_op jit(solution)/shard_map/all_gather | solution.py:287
  8.7 171.2 %all-gather.9.cloned.1.call-start = ((), (), s32[]{:S(2)}) async-start(), calls=%async_computation.15 | async-start | bytes 1216512 | tf_op jit(solution)/shard_map/all_gather | solution.py:286
  9.4 226.3 %all-gather.13.cloned.1.call-start = ((), (), s32[]{:S(2)}) async-start(), calls=%async_computation.17 | async-start | bytes 1216512 | tf_op jit(solution)/shard_map/all_gather | solution.py:289
  10.0 291.1 %all-gather.15.cloned.1.call-start = ((), (), s32[]{:S(2)}) async-start(), calls=%async_computation.18 | async-start | bytes 4866048 | tf_op jit(solution)/shard_map/all_gather | solution.py:293
  10.6 355.7 %all-gather.17.cloned.1.call-start = ((), (), s32[]{:S(2)}) async-start(), calls=%async_computation.19 | async-start | bytes 4866048 | tf_op jit(solution)/shard_map/all_gather | solution.py:295
  11.2 621.9 %reduce-scatter.13.cloned.1.call-start = ((), (), s32[]{:S(2)}) async-start(), calls=%async_computation.23 | async-start | bytes 2433024 | tf_op jit(solution)/shard_map/reduce_scatter | solution.py:334
  68.2 167.5 %copy-start.4 = (bf16[2,256,768]{2,1,0:T(8,128)(2,1)}, bf16[2,256,768]{2,1,0:T(8,128)(2,1)S(1)}, u32[]{:S(2)}) copy-start(bf16[2,256,768]{2,1,0:T(8,128)(2,1)S(1)} %copy.171) | copy-start | bytes 2359300
  218.1 9.6 copy-start
  218.1 9.6 copy-start.48
  218.1 9.6 copy-start.87
  227.8 11.2 %copy-start.30 = (bf16[64,8,2,384]{3,1,2,0:T(8,128)(2,1)}, bf16[64,8,2,384]{3,1,2,0:T(8,128)(2,1)S(1)}, u32[]{:S(2)}) copy-start(bf16[64,8,2,384]{3,1,2,0:T(8,128)(2,1)S(1)} %copy.225) | copy-start | bytes 2359300
  239.1 158.9 %copy-start.72 = (f32[512]{0:T(512)}, f32[512]{0:T(512)S(1)}, u32[]{:S(2)}) copy-start(f32[512]{0:T(512)S(1)} %broadcast_multiply_fusion.9) | copy-start | bytes 6148
  239.1 4.0 copy-start.25
  287.5 9.9 copy-start.2
  287.5 10.0 copy-start.46
  287.6 10.0 copy-start.85
  290.9 6.8 copy-start.94
  298.6 104.1 %copy-start.6 = (f32[512,768]{1,0:T(8,128)}, f32[512,768]{1,0:T(8,128)S(1)}, u32[]{:S(2)}) copy-start(f32[512,768]{1,0:T(8,128)S(1)} %get-tuple-element.458) | copy-start | bytes 4718596
  298.6 104.0 %copy-start.57 = (f32[512]{0:T(512)}, f32[512]{0:T(512)S(1)}, u32[]{:S(2)}) copy-start(f32[512]{0:T(512)S(1)} %broadcast_multiply_fusion.7) | copy-start | bytes 6148
  300.0 97.9 %copy-start.82 = (f32[512]{0:T(512)}, f32[512]{0:T(512)S(1)}, u32[]{:S(2)}) copy-start(f32[512]{0:T(512)S(1)} %add_rsqrt_fusion.3) | copy-start | bytes 6148
  300.0 102.6 %copy-start.59 = (f32[512]{0:T(512)}, f32[512]{0:T(512)S(1)}, u32[]{:S(2)}) copy-start(f32[512]{0:T(512)S(1)} %add_rsqrt_fusion.1) | copy-start | bytes 6148
  300.0 8.5 copy-start.44
  300.1 8.5 copy-start.69
  301.1 7.5 copy-start.89
  308.6 57.7 %copy-start.81 = (f32[768]{0:T(1024)S(1)}, f32[768]{0:T(1024)}, u32[]{:S(2)}) copy-start(f32[768]{0:T(1024)} %convert_element_type.278) | copy-start | bytes 9220
  366.3 6.5 copy-start.27
  366.3 6.5 copy-start.90
  372.4 9.3 slice-start.2
  372.8 9.0 slice-start.3
  378.8 8.3 slice-start
  381.8 5.3 copy-start.22
  381.8 16.2 %copy-start.20 = (f32[512,768]{1,0:T(8,128)}, f32[512,768]{1,0:T(8,128)S(1)}, u32[]{:S(2)}) copy-start(f32[512,768]{1,0:T(8,128)S(1)} %get-tuple-element.397) | copy-start | bytes 4718596
  381.8 5.3 slice-start.1
  390.7 7.3 copy-start.45
  397.9 3.9 copy-start.28
  398.0 3.9 copy-start.31
  401.8 5.5 copy-start.23
  416.1 4.3 copy-start.1
  416.1 4.3 copy-start.49
  416.1 4.3 copy-start.88
  442.9 7.1 copy-start.12
  442.9 7.1 copy-start.95
  455.8 33.8 %all-to-all-start.5 = ((bf16[2,3,512,384]{3,0,1,2:T(2,128)(2,1)}), bf16[2,3,512,384]{3,0,1,2:T(2,128)(2,1)}, u32[]{:S(2)}, u32[]{:S(2)}) async-start(bf16[2,3,512,384]{3,0,1,2:T(2,128)(2,1)} %copy.187), calls=%async_computation.5 | async-start | bytes 4718592 | tf_op jit(solution)/shard_map/all_to_all | solution.py:211
  460.7 172.4 %reduce-scatter.11.cloned.1.call-start = ((), (), s32[]{:S(2)}) async-start(), calls=%async_computation.22 | async-start | bytes 2433024 | tf_op jit(solution)/shard_map/reduce_scatter | solution.py:332
  462.4 4.7 copy-start.3
  462.4 4.7 copy-start.47
  462.4 4.7 copy-start.86
  523.6 202.4 %reduce-scatter.9.cloned.1.call-start = ((), (), s32[]{:S(2)}) async-start(), calls=%async_computation.21 | async-start | bytes 2433024 | tf_op jit(solution)/shard_map/reduce_scatter | solution.py:331
  531.8 298.8 %reduce-scatter.7.cloned.1.call-start = ((), (), s32[]{:S(2)}) async-start(), calls=%async_computation.20 | async-start | bytes 2433024 | tf_op jit(solution)/shard_map/reduce_scatter | solution.py:329
  540.0 5.4 copy-start.21
  540.0 431.7 %reduce-scatter.17.cloned.1.call-start = ((), (), s32[]{:S(2)}) async-start(), calls=%async_computation.25 | async-start | bytes 9732096 | tf_op jit(solution)/shard_map/reduce_scatter | solution.py:340
  540.0 5.3 copy-start.19
  550.7 6.2 copy-start.7
  550.7 6.2 copy-start.58
  550.7 6.2 copy-start.60
  550.7 562.9 %reduce-scatter.15.cloned.1.call-start = ((), (), s32[]{:S(2)}) async-start(), calls=%async_computation.24 | async-start | bytes 9732096 | tf_op jit(solution)/shard_map/reduce_scatter | solution.py:338
  551.4 5.5 copy-start.29
  562.7 3.7 copy-start.63
  562.8 3.7 copy-start.64
  564.6 49.4 %copy-start.42 = (bf16[2,1,256,768]{3,2,0,1:T(8,128)(2,1)S(1)}, bf16[2,1,256,768]{3,2,0,1:T(8,128)(2,1)}, u32[]{:S(2)}) copy-start(bf16[2,1,256,768]{3,2,0,1:T(8,128)(2,1)} %copy.191) | copy-start | bytes 2359300
  628.0 3.8 copy-start.40
  628.0 3.8 copy-start.41
  (51 other events, 92.0 us)
Sparse Core Ops, SparseCore 0:
  10.9 56.9 all-gather.6
  70.8 53.1 all-gather.10
  126.9 52.9 all-gather.8
  182.7 52.9 all-gather.12
  238.5 62.5 all-gather.14
  303.8 62.4 all-gather.16
  407.4 97.9 reduce-scatter.12
  523.7 98.2 reduce-scatter.10
  627.9 98.0 reduce-scatter.8
  732.6 97.9 reduce-scatter.6
  837.1 134.6 reduce-scatter.16
  979.1 134.5 reduce-scatter.14
where the time goes:
time: 1130 us; the launch traced here: 1120 us
  waiting for transfers between devices  619 us (55%)
  matrix products  171 us (15%)
  local copies, waits for them, and re-layouts  128 us (11%)
  blocking collectives  125 us (11%)
  other arithmetic  55.9 us (5%)
  between operations  16.1 us (1%)
    reduce_scatter x1, waiting for transfers between devices, per_device(): lax.psum_scatter(grad_iweight, ('seq', 'fsdp'), scatter_dimension=0, tile...  142 us
    reduce_scatter x1, waiting for transfers between devices, per_device(): lax.psum_scatter(grad_uweight, ('seq', 'fsdp'), scatter_dimension=0, tile...  141 us
    reduce_scatter x1, waiting for transfers between devices, per_device(): lax.psum_scatter(grad_qweight, ('seq', 'fsdp'), scatter_dimension=0, tile...  105 us
    reduce_scatter x1, waiting for transfers between devices, per_device(): lax.psum_scatter(grad_kweight, ('seq', 'fsdp'), scatter_dimension=0, tile...  93 us
    unnamed x2, blocking collectives  83 us
    all_gather x1, waiting for transfers between devices, per_device(): lax.all_gather(key_weight, ('seq', 'fsdp'), axis=0, tiled=True)  53.2 us
    all_gather x1, waiting for transfers between devices, per_device(): lax.all_gather(value_weight, ('seq', 'fsdp'), axis=0, tiled=True)  46.6 us
    dot_general x2, matrix products, micro_pass(): jnp.dot(first_low, inner_weight, preferred_element_type=jnp.float32)  36.3 us
  transfers between devices with their start and end apart: 13, of which 9 were waited for; matrix products, arithmetic and copies ran while one was open for 26% of the time, Pallas kernels for 0%

commit v1 on v0

v1 whole, which is shorter than its diff:
```python
import math

import jax
import jax.numpy as jnp
from jax import lax
from jax.experimental import pallas as pl
from jax.experimental.pallas import tpu as pltpu
from jax.sharding import PartitionSpec as P

HD = 64
MEM = 10
SEG = 512
BF = jnp.bfloat16
F32 = jnp.float32

EPSILON = 1e-12
ROOT_HALF = math.sqrt(0.5)
INV_ROOT_TAU = 1.0 / math.sqrt(2.0 * math.pi)
AXES = ("seq", "fsdp")


def normalize(resid):
    centre = resid - jnp.mean(resid, axis=-1, keepdims=True)
    inverse = lax.rsqrt(jnp.mean(centre * centre, axis=-1, keepdims=True) + EPSILON)
    return (centre * inverse, inverse)


def norm_back(grad_out, normed, inverse, gain):
    scaled = grad_out * gain
    return inverse * (
        scaled
        - jnp.mean(scaled, axis=-1, keepdims=True)
        - normed * jnp.mean(scaled * normed, axis=-1, keepdims=True)
    )


def gelu_slope(inner):
    return (
        0.5 * (1.0 + lax.erf(inner * ROOT_HALF))
        + inner * jnp.exp(-0.5 * inner * inner) * INV_ROOT_TAU
    )


def dot(a, b):
    return jnp.dot(a, b, preferred_element_type=F32)


def dot_nt(a, b):
    return lax.dot_general(a, b, (((1,), (1,)), ((), ())), preferred_element_type=F32)


def dot_tn(a, b):
    return lax.dot_general(a, b, (((0,), (0,)), ((), ())), preferred_element_type=F32)


def hop(x, bit):
    size = lax.axis_size("fsdp")
    return lax.ppermute(x, "fsdp", [(i, i ^ bit) for i in range(size)])


def hop_core(x):
    return lax.ppermute(x, "seq", [(0, 1), (1, 0)])


ORDER_A = [b + x + y for y in (0, 2) for x in (0, 1) for b in (0, 4, 8, 12)]
ORDER_B = [b + x + y for x in (0, 1) for y in (0, 2) for b in (0, 4, 8, 12)]


def place_kernel(a_ref, b_ref, ac_ref, bc_ref, out_ref, sem):
    side = lax.axis_index("seq")
    me = lax.axis_index("fsdp")
    half = a_ref.shape[1]
    copies = []
    for order, low, mine, other in (
        (ORDER_A, 0, a_ref, ac_ref),
        (ORDER_B, half, b_ref, bc_ref),
    ):
        for j, bits in enumerate(order):
            at = jnp.bitwise_xor(me, bits)
            for src, core in ((mine, side), (other, 1 - side)):
                copies.append(
                    pltpu.make_async_copy(
                        src.at[j],
                        out_ref.at[core * 16 + at, low : low + half],
                        sem.at[len(copies)],
                    )
                )
    for copy in copies:
        copy.start()
    for copy in copies:
        copy.wait()


def gather_group(x):
    half = x.shape[0] // 2
    z = jnp.stack([x] + [hop(x, b) for b in (4, 8, 12)])
    a, b = z[:, :half], z[:, half:]
    ax, by = hop(a, 1), hop(b, 2)
    a2, b2 = jnp.concatenate([a, ax]), jnp.concatenate([b, by])
    ay, bx = hop(a2, 2), hop(b2, 1)
    a3, b3 = jnp.concatenate([a2, ay]), jnp.concatenate([b2, bx])
    ac, bc = hop_core(a3), hop_core(b3)
    shape = (32,) + x.shape
    return pl.pallas_call(
        place_kernel,
        out_shape=jax.ShapeDtypeStruct(shape, x.dtype),
        in_specs=[pl.BlockSpec(memory_space=pl.ANY)] * 4,
        out_specs=pl.BlockSpec(memory_space=pl.ANY),
        scratch_shapes=[pltpu.SemaphoreType.DMA((64,))],
        cost_estimate=pl.CostEstimate(
            flops=0, transcendentals=0, bytes_accessed=128 * x.size
        ),
    )(a3, b3, ac, bc)


def part(x, index, axis):
    return lax.dynamic_index_in_dim(x, index, axis, keepdims=False)


def add_low(*terms):
    total = terms[0].astype(F32)
    for term in terms[1:]:
        total = total + term.astype(F32)
    return total.astype(BF)


def scatter_group(g):
    side = lax.axis_index("seq")
    me = lax.axis_index("fsdp")
    zi, yi, xi = me // 4, (me // 2) % 2, me % 2
    units = g.shape[1]
    half = units // 2
    g = g.reshape((2, 4, 2, 2) + g.shape[1:])
    got = hop_core(part(g, 1 - side, 0))
    s = add_low(part(g, side, 0), got)
    a, b = s[:, :, :, :half], s[:, :, :, half:]
    ga, gb = hop(part(a, 1 - yi, 1), 2), hop(part(b, 1 - xi, 2), 1)
    a, b = add_low(part(a, yi, 1), ga), add_low(part(b, xi, 2), gb)
    ga, gb = hop(part(a, 1 - xi, 1), 1), hop(part(b, 1 - yi, 1), 2)
    s = jnp.concatenate(
        [add_low(part(a, xi, 1), ga), add_low(part(b, yi, 1), gb)], axis=1
    )
    got = [hop(part(s, jnp.bitwise_xor(zi, d), 0), 4 * d) for d in (1, 2, 3)]
    total = part(s, zi, 0).astype(F32)
    for term in got:
        total = total + term.astype(F32)
    return total


def key_keep(valid):
    places = jnp.arange(SEG)
    return (places < MEM) | (places >= SEG - MEM) | (places - MEM < valid)


def head_split(block):
    return block.reshape(block.shape[0], -1, HD)


def segment_scores(query, keys, valid):
    query_h = head_split(query)
    keys_h = head_split(keys)
    scores = jnp.einsum(
        "qhe,khe->hqk", query_h, keys_h, preferred_element_type=F32
    ) * HD ** (-0.5)
    keep = key_keep(valid)
    return jnp.where(keep[None, None, :], scores, -1000000000.0), query_h, keys_h


def attend_segment(query, keys, values, valid):
    scores, _, _ = segment_scores(query, keys, valid)
    top = jnp.max(scores, axis=-1, keepdims=True)
    weights = jnp.exp(scores - top)
    total = jnp.sum(weights, axis=-1, keepdims=True)
    probs = weights / total
    mixed = jnp.einsum(
        "hqk,khe->qhe", probs.astype(BF), head_split(values), preferred_element_type=F32
    )
    return mixed.reshape(SEG, -1).astype(BF), (top + jnp.log(total))[..., 0]


def attend_back(query, keys, values, grad_mixed, log_total, valid):
    scores, query_h, keys_h = segment_scores(query, keys, valid)
    probs = jnp.exp(scores - log_total[..., None])
    grad_h = head_split(grad_mixed)
    grad_probs = jnp.einsum(
        "qhe,khe->hqk", grad_h, head_split(values), preferred_element_type=F32
    )
    delta = jnp.sum(probs * grad_probs, axis=-1, keepdims=True)
    grad_scores = (probs * (grad_probs - delta)).astype(BF)
    scale = HD ** (-0.5)
    grad_query = (
        jnp.einsum("hqk,khe->qhe", grad_scores, keys_h, preferred_element_type=F32)
        * scale
    )
    grad_keys = (
        jnp.einsum("hqk,qhe->khe", grad_scores, query_h, preferred_element_type=F32)
        * scale
    )
    grad_values = jnp.einsum(
        "hqk,qhe->khe", probs.astype(BF), grad_h, preferred_element_type=F32
    )
    return tuple(
        g.reshape(SEG, -1).astype(BF) for g in (grad_query, grad_keys, grad_values)
    )


def column_sum(values):
    return jnp.sum(values.astype(F32), axis=0)


VECTORS = (
    "query_bias",
    "value_bias",
    "output_bias",
    "first_gain",
    "first_shift",
    "outer_bias",
    "second_gain",
    "second_shift",
)


def split_columns(w, width):
    return jnp.stack([w[:, i : i + width] for i in range(0, w.shape[1], width)])


def gather_params(p, ring):
    if not ring:
        full = {
            name: lax.all_gather(value, AXES, axis=0, tiled=True)
            for name, value in p.items()
        }
        return full
    width = p["query_weight"].shape[1]
    rows = p["query_weight"].shape[0]
    vec = jnp.concatenate([p[n] for n in VECTORS] + [p["inner_bias"]])
    room = rows * width
    vec = jnp.pad(vec, (0, width - vec.shape[0])).reshape(1, width)
    vec = jnp.pad(vec, ((0, rows - 1), (0, 0)))
    del room
    first = gather_group(
        jnp.stack([p["query_weight"], p["key_weight"], p["value_weight"], vec])
    )
    second = gather_group(
        jnp.concatenate(
            [p["output_weight"][None], split_columns(p["inner_weight"], width),
             jnp.zeros((1, rows, width), BF)]
        )
    )
    third = gather_group(p["outer_weight"].reshape(4, -1, width))
    full = {}
    for i, name in enumerate(("query_weight", "key_weight", "value_weight")):
        full[name] = first[:, i].reshape(-1, width)
    got = first[:, 3, 0]
    for i, name in enumerate(VECTORS):
        full[name] = got[:, i * rows : (i + 1) * rows].reshape(-1)
    at = len(VECTORS) * rows
    full["inner_bias"] = got[:, at : at + p["inner_bias"].shape[0]].reshape(-1)
    full["output_weight"] = second[:, 0].reshape(-1, width)
    full["inner_weight"] = jnp.concatenate(
        [second[:, 1 + i].reshape(-1, width) for i in range(4)], axis=1
    )
    full["outer_weight"] = third.reshape(-1, width)
    return full


def layer_pass(w, rows, cot, valid):
    count, seg, width = rows.shape
    flat = rows.reshape(-1, width)
    query = (dot(flat, w["query_weight"]) + w["query_bias"].astype(F32)).astype(BF)
    keys = dot(flat, w["key_weight"]).astype(BF)
    values = (dot(flat, w["value_weight"]) + w["value_bias"].astype(F32)).astype(BF)
    mixed, logs = [], []
    for s in range(count):
        cut = slice(s * seg, (s + 1) * seg)
        m, lt = attend_segment(query[cut], keys[cut], values[cut], valid[s])
        mixed.append(m)
        logs.append(lt)
    attended = jnp.concatenate(mixed)
    branch = dot(attended, w["output_weight"]) + w["output_bias"].astype(F32)
    normed_one, inverse_one = normalize(flat.astype(F32) + branch)
    first = normed_one * w["first_gain"].astype(F32) + w["first_shift"].astype(F32)
    first_low = first.astype(BF)
    inner = dot(first_low, w["inner_weight"]) + w["inner_bias"].astype(F32)
    active = jax.nn.gelu(inner, approximate=False).astype(BF)
    outer = dot(active, w["outer_weight"]) + w["outer_bias"].astype(F32)
    normed_two, inverse_two = normalize(first + outer)
    result = (
        normed_two * w["second_gain"].astype(F32) + w["second_shift"].astype(F32)
    ).astype(BF)
    grad_out = cot.reshape(-1, width).astype(F32)
    g = {}
    g["second_gain"] = jnp.sum(grad_out * normed_two, axis=0)
    g["second_shift"] = jnp.sum(grad_out, axis=0)
    grad_res_two = norm_back(
        grad_out, normed_two, inverse_two, w["second_gain"].astype(F32)
    )
    grad_outer = grad_res_two.astype(BF)
    g["outer_bias"] = column_sum(grad_outer)
    g["outer_weight"] = dot_tn(active, grad_outer)
    grad_active = dot_nt(grad_outer, w["outer_weight"])
    grad_inner = (grad_active * gelu_slope(inner)).astype(BF)
    g["inner_bias"] = column_sum(grad_inner)
    g["inner_weight"] = dot_tn(first_low, grad_inner)
    grad_first = grad_res_two + dot_nt(grad_inner, w["inner_weight"])
    g["first_gain"] = jnp.sum(grad_first * normed_one, axis=0)
    g["first_shift"] = jnp.sum(grad_first, axis=0)
    grad_res_one = norm_back(
        grad_first, normed_one, inverse_one, w["first_gain"].astype(F32)
    )
    grad_branch = grad_res_one.astype(BF)
    g["output_bias"] = column_sum(grad_branch)
    g["output_weight"] = dot_tn(attended, grad_branch)
    grad_attended = dot_nt(grad_branch, w["output_weight"]).astype(BF)
    parts = []
    for s in range(count):
        cut = slice(s * seg, (s + 1) * seg)
        parts.append(
            attend_back(
                query[cut], keys[cut], values[cut], grad_attended[cut], logs[s], valid[s]
            )
        )
    grad_query, grad_keys, grad_values = (
        jnp.concatenate([q[i] for q in parts]) for i in range(3)
    )
    g["query_weight"] = dot_tn(flat, grad_query)
    g["query_bias"] = column_sum(grad_query)
    g["key_weight"] = dot_tn(flat, grad_keys)
    g["value_weight"] = dot_tn(flat, grad_values)
    g["value_bias"] = column_sum(grad_values)
    grad_rows = (
        grad_res_one
        + dot_nt(grad_query, w["query_weight"])
        + dot_nt(grad_keys, w["key_weight"])
        + dot_nt(grad_values, w["value_weight"])
    )
    return (
        result.reshape(rows.shape),
        grad_rows.reshape(rows.shape),
        g,
    )


NAMES = (
    "query_weight",
    "query_bias",
    "key_weight",
    "value_weight",
    "value_bias",
    "output_weight",
    "output_bias",
    "first_gain",
    "first_shift",
    "inner_weight",
    "inner_bias",
    "outer_weight",
    "outer_bias",
    "second_gain",
    "second_shift",
)


def scatter_params(g, ring):
    if not ring:
        return {
            name: lax.psum_scatter(value, AXES, scatter_dimension=0, tiled=True)
            for name, value in g.items()
        }
    width = g["query_weight"].shape[1]
    low = {n: v.astype(BF) for n, v in g.items()}
    rows = width // 32
    out = {}
    out["outer_weight"] = scatter_group(
        low["outer_weight"].reshape(32, 4, -1, width)
    ).reshape(-1, width)
    inner = jnp.stack(
        [
            low["inner_weight"][:, i * width : (i + 1) * width].reshape(32, rows, width)
            for i in range(4)
        ],
        axis=1,
    )
    got = scatter_group(inner)
    out["inner_weight"] = jnp.concatenate([got[i] for i in range(4)], axis=1)
    vec = jnp.concatenate(
        [low[n].reshape(32, -1) for n in VECTORS] + [low["inner_bias"].reshape(32, -1)],
        axis=1,
    )
    used = vec.shape[1]
    vec = jnp.pad(vec, ((0, 0), (0, width - used))).reshape(32, 1, 1, width)
    vec = jnp.pad(vec, ((0, 0), (0, 0), (0, rows - 1), (0, 0)))
    names = ("output_weight", "value_weight", "key_weight", "query_weight")
    stack = jnp.stack([low[n].reshape(32, rows, width) for n in names], axis=1)
    got = scatter_group(jnp.concatenate([stack, vec, jnp.zeros_like(vec)], axis=1))
    for i, n in enumerate(names):
        out[n] = got[i]
    got = got[4, 0]
    for i, n in enumerate(VECTORS):
        out[n] = got[i * rows : (i + 1) * rows]
    at = len(VECTORS) * rows
    out["inner_bias"] = got[at:used]
    return out


def per_device(tokens, read_memory, valid_count, cotangent, *params):
    side = lax.axis_index("seq")
    ring = lax.axis_size("fsdp") == 16
    p = dict(zip(NAMES, params))
    half = tokens.shape[0] // 2
    near = side * half
    far = (1 - side) * half

    def take(x, at):
        return lax.dynamic_slice_in_dim(x, at, half, axis=0)

    def merge(x):
        own, got = take(x, near), hop_core(take(x, far))
        return jnp.where(side == 0, own, got), jnp.where(side == 0, got, own)

    mem = take(read_memory, near)
    valid = take(valid_count, near)
    low_tok, high_tok = merge(tokens)
    rows = jnp.concatenate([mem, low_tok, high_tok, mem], axis=1)
    cot = jnp.concatenate(merge(cotangent), axis=1)

    full = gather_params(p, ring)
    result, grad_rows, grads = layer_pass(full, rows, cot, valid)

    def back(low, high):
        own = jnp.where(side == 0, low, high)
        got = hop_core(jnp.where(side == 0, high, low))
        return jnp.concatenate(
            [jnp.where(side == 0, own, got), jnp.where(side == 0, got, own)]
        )

    mid = SEG // 2
    layer_out = back(result[:, :mid], result[:, mid:])
    grad_low = grad_rows.astype(BF)
    tokens_grad = back(grad_low[:, MEM:mid], grad_low[:, mid : SEG - MEM])
    grad_mem = grad_rows[:, :MEM] + grad_rows[:, SEG - MEM :]
    got = hop_core(grad_mem)
    memory_grad = jnp.concatenate(
        [jnp.where(side == 0, grad_mem, got), jnp.where(side == 0, got, grad_mem)]
    )
    shards = scatter_params(grads, ring)
    return (layer_out, tokens_grad, memory_grad) + tuple(shards[n] for n in NAMES)


def solution(mesh):
    row = P("fsdp", "seq", None)
    whole = P("fsdp", None, None)
    mat, vec = P(AXES, None), P(AXES)
    specs = tuple(mat if n.endswith("_weight") else vec for n in NAMES)
    return jax.shard_map(
        per_device,
        mesh=mesh,
        in_specs=(row, whole, P("fsdp"), row) + specs,
        out_specs=(row, row, whole) + specs,
        check_vma=False,
    )
```

time: 1130 us -> 1010 us (0.89)
  Pallas kernels: 0 us -> 505 us
  waiting for transfers between devices: 619 us -> 130 us
  blocking collectives: 125 us -> 0 us
  local copies, waits for them, and re-layouts: 128 us -> 64.6 us
  starting transfers between devices: 5.57 us -> 62.3 us
  between operations: 16.1 us -> 2.54 us
    pallas_call x0 -> x3, Pallas kernels: none -> 505 us  [gather_group(): pl.pallas_call(place_kernel, out_shape=jax.ShapeDtypeStruct(shape, x.dtyp...]
    reduce_scatter x6 -> x0, waiting for transfers between devices: 481 us -> none  [the longest x1 142 us: per_device(): lax.psum_scatter(grad_iweight, ('seq', 'fsdp'), scatter_dimension=0, tile...]
    all_gather x6 -> x0, waiting for transfers between devices: 135 us -> none  [the longest x1 53.2 us: per_device(): lax.all_gather(key_weight, ('seq', 'fsdp'), axis=0, tiled=True)]
    ppermute x0 -> x56, waiting for transfers between devices: none -> 130 us  [the longest x42 124 us: hop(): return lax.ppermute(x, 'fsdp', [(i, i ^ bit) for i in range(size)])]
    unnamed x2 -> x0, blocking collectives: 83 us -> none
    ppermute x0 -> x56, starting transfers between devices: none -> 62.3 us  [the longest x42 59.7 us: hop(): return lax.ppermute(x, 'fsdp', [(i, i ^ bit) for i in range(size)])]
    all_to_all x14 -> x0, local copies, waits for them, and re-layouts: 39.7 us -> none  [the longest x4 18.3 us: micro_pass(): lax.all_to_all(stacked, 'seq', split_axis=3, concat_axis=2, tiled=True)]
    all_to_all x7 -> x0, blocking collectives: 37.7 us -> none  [the longest x2 11.8 us: micro_pass(): lax.all_to_all(stacked, 'seq', split_axis=3, concat_axis=2, tiled=True)]
  transfers between devices with their start and end apart: 13 -> 56, of which waited for: 9 -> 21; matrix products, arithmetic and copies ran while one was open for 26% -> 10% of each run, Pallas kernels for 0% -> 29%
where the time goes in v1:
time: 1010 us; the launch traced here: 1000 us
  Pallas kernels  505 us (50%)
  matrix products  172 us (17%)
  waiting for transfers between devices  130 us (13%)
  other arithmetic  66.1 us (7%)
  local copies, waits for them, and re-layouts  64.6 us (6%)
  starting transfers between devices  62.3 us (6%)
    pallas_call x3, Pallas kernels, gather_group(): pl.pallas_call(place_kernel, out_shape=jax.ShapeDtypeStruct(shape, x.dtyp...  505 us
    ppermute x42, waiting for transfers between devices, hop(): return lax.ppermute(x, 'fsdp', [(i, i ^ bit) for i in range(size)])  124 us
    dot_general x6, matrix products, dot(): return jnp.dot(a, b, preferred_element_type=F32)  66.9 us
    ppermute x42, starting transfers between devices, hop(): return lax.ppermute(x, 'fsdp', [(i, i ^ bit) for i in range(size)])  59.7 us
    dot_general x6, matrix products, dot_nt(): lax.dot_general(a, b, (((1,), (1,)), ((), ())), preferred_element_type=F32)  29.9 us
    unnamed x184, local copies, waits for them, and re-layouts  28.7 us
    dot_general x6, matrix products, dot_tn(): lax.dot_general(a, b, (((0,), (0,)), ((), ())), preferred_element_type=F32)  23.9 us
  transfers between devices with their start and end apart: 56, of which 21 were waited for; matrix products, arithmetic and copies ran while one was open for 10% of the time, Pallas kernels for 29%

profile of v1, /device:TPU:0, one launch (start us, length us, event | category | flops | bytes accessed | tf_op | source)
XLA Modules:
  0.0 1002.2 jit_solution(15989558593954477935)
XLA Ops:
  0.7 6.1 concatenate.109
  7.7 3.1 collective-permute-start.1
  10.8 2.6 collective-permute-start.2
  20.0 4.4 constant_dynamic-slice_fusion.8
  26.6 2.5 collective-permute-start.11
  34.0 25.0 %collective-permute-done.20 = bf16[4,24,768]{2,1,0:T(8,128)(2,1)S(1)} collective-permute-done((bf16[4,24,768]{2,1,0:T(8,128)(2,1)S(1)}, bf16[4,24,768]{2,1,0:T(8,128)(2,1)S(1)}, u32[]{:S(2)}, u32[]{:S(2)}) %collective-permute-start.20) | collective-permute-done | bytes 147488 | tf_op jit(solution)/shard_map/ppermute | solution.py:58
  65.0 3.9 collective-permute-done.6
  76.7 3.5 collective-permute-done.24
  81.8 4.6 collective-permute-done.13
  89.8 2.1 pad_maximum_fusion.27
  91.9 4.0 collective-permute-done.7
  101.5 7.6 collective-permute-done.23
  112.4 2.5 pad_maximum_fusion.14.a_ref
  114.9 2.3 pad_maximum_fusion.15.b_ref
  117.2 8.5 collective-permute-done.16
  125.7 2.7 pad_maximum_fusion.3.b_ref
  128.9 2.7 pad_maximum_fusion.2.a_ref
  131.6 144.6 %shard_map.322 = bf16[32,4,24,768]{3,2,1,0:T(8,128)(2,1)} custom-call(bf16[16,2,24,768]{3,2,1,0:T(8,128)(2,1)} %pad_maximum_fusion.12.a_ref, bf16[16,2,24,768]{3,2,1,0:T(8,128)(2,1)} %copy-done.18, bf16[16,2,24,768]{3,2,1,0:T(8,128)(2,1)} %collective-permute-done.8.ac_ref, bf16[16,2,24,768]{3,2,1,0:T(8,128)(2,1)} %collective-permute-done.9.bc_ref), custom_call_target="tpu_custom_call" | custom-call | bytes 9437184 | tf_op jit(solution)/shard_map/pallas_call | solution.py:104
  277.3 4.0 fusion.120
  281.6 2.7 add_convert_fusion.1
  287.9 3.9 add_convert_fusion.2
  293.2 3.0 fusion.133
  300.8 3.2 fusion.48
  304.1 3.0 fusion.132
  309.4 2.3 copy-done.3
  312.9 144.6 %shard_map.324 = bf16[32,4,24,768]{3,2,1,0:T(8,128)(2,1)} custom-call(bf16[16,2,24,768]{3,2,1,0:T(8,128)(2,1)} %pad_maximum_fusion.14.a_ref, bf16[16,2,24,768]{3,2,1,0:T(8,128)(2,1)} %pad_maximum_fusion.15.b_ref, bf16[16,2,24,768]{3,2,1,0:T(8,128)(2,1)} %collective-permute-done.26.ac_ref, bf16[16,2,24,768]{3,2,1,0:T(8,128)(2,1)} %collective-permute-done.27.bc_ref), custom_call_target="tpu_custom_call" | custom-call | bytes 9437184 | tf_op jit(solution)/shard_map/pallas_call | solution.py:104
  457.6 7.8 fusion.47
  465.3 216.1 %shard_map.323 = bf16[32,6,24,768]{3,2,1,0:T(8,128)(2,1)} custom-call(bf16[16,3,24,768]{3,2,1,0:T(8,128)(2,1)} %pad_maximum_fusion.2.a_ref, bf16[16,3,24,768]{3,2,1,0:T(8,128)(2,1)} %pad_maximum_fusion.3.b_ref, bf16[16,3,24,768]{3,2,1,0:T(8,128)(2,1)} %collective-permute-done.17.ac_ref, bf16[16,3,24,768]{3,2,1,0:T(8,128)(2,1)} %collective-permute-done.18.bc_ref), custom_call_target="tpu_custom_call" | custom-call | bytes 14155776 | tf_op jit(solution)/shard_map/pallas_call | solution.py:104
  681.5 4.8 fusion.118
  689.6 49.6 %fusion.2 = (bf16[1024,3072]{1,0:T(8,128)(2,1)}, f32[1024,3072]{1,0:T(8,128)}) fusion(f32[3072]{0:T(1024)S(1)} %reshape.396, bf16[768,768]{1,0:T(8,128)(2,1)S(1)} %bitcast.362, bf16[768,768]{1,0:T(8,128)(2,1)S(1)} %bitcast.364, bf16[768,768]{1,0:T(8,128)(2,1)S(1)} %bitcast.366, bf16[768,768]{1,0:T(8,128)(2,1)} %bitcast.368, ...), kind=kOutput, calls=%fused_computation.4 | convolution fusion | flops 5062262784 | bytes 26765312 | tf_op jit(solution)/shard_map/dot_general | solution.py:45
  739.2 7.5 fusion.135
  747.3 2.8 fusion.37
  751.7 7.0 convolution_convert_fusion
  758.8 11.6 %fusion.140 = (bf16[3072]{0:T(1024)(128)(2,1)S(1)}, bf16[1024,3072]{1,0:T(8,128)(2,1)S(1)}) fusion(f32[1024,3072]{1,0:T(8,128)} %get-tuple-element.145, f32[3072]{0:T(1024)S(1)} %reshape.396, bf16[3072,768]{1,0:T(8,128)(2,1)S(1)} %bitcast.337, f32[1024,768]{1,0:T(8,128)S(1)} %get-tuple-element.47), kind=kOutput, calls=%fused_computation.353 | convolution fusion | flops 4870370304 | bytes 26757120 | tf_op jit(solution)/shard_map/dot_general | solution.py:49
  770.4 2.6 copy-done.65
  773.0 8.1 convolution_convert_fusion.1
  781.2 8.9 multiply_reduce_fusion.2
  796.7 3.0 fusion.138
  799.7 8.9 multiply_reduce_fusion.1
  808.6 4.1 fusion.139
  812.7 8.7 multiply_reduce_fusion
  821.4 10.1 %multiply_convert_fusion.1 = bf16[12,512,512]{1,2,0:T(8,128)(2,1)} fusion(f32[12,512,512]{1,2,0:T(8,128)} %get-tuple-element.152, f32[12,512,512]{1,2,0:T(8,128)S(1)} %bitcast.302, f32[12,512]{1,0:T(8,128)S(1)} %get-tuple-element.151, f32[12,512]{1,0:T(8,128)S(1)} %copy-done.57), kind=kLoop, calls=%fused_computation.14 | loop fusion | flops 12582912 | bytes 31506432 | tf_op jit(solution)/shard_map/convert_element_type | solution.py:189
  831.5 4.1 fusion.136
  838.3 7.0 multiply_convert_fusion
  848.8 2.4 convolution_convert_fusion.7
  851.2 2.5 convolution_convert_fusion.4
  853.7 3.1 fusion.55
  856.8 2.4 convolution_convert_fusion.5
  859.2 3.1 fusion.54
  880.8 5.4 collective-permute-done.31
  890.8 2.4 fusion.29
  895.1 2.3 fusion.30
  901.4 8.4 collective-permute-done.51
  910.7 11.0 %collective-permute-done.43 = bf16[4,2,2,24,768]{4,3,2,0,1:T(8,128)(2,1)S(1)} collective-permute-done((bf16[4,2,2,24,768]{4,3,2,0,1:T(8,128)(2,1)S(1)}, bf16[4,2,2,24,768]{4,3,2,0,1:T(8,128)(2,1)S(1)}, u32[]{:S(2)}, u32[]{:S(2)}) %collective-permute-start.43) | collective-permute-done | bytes 589856 | tf_op jit(solution)/shard_map/ppermute | solution.py:58
  922.5 5.6 collective-permute-done.41
  930.6 9.0 collective-permute-done.44
  939.9 6.4 collective-permute-start.45
  954.7 5.0 collective-permute-done.46
  960.5 3.1 collective-permute-start.55
  963.8 7.8 collective-permute-done.35
  976.3 5.2 collective-permute-done.36
  983.9 2.4 collective-permute-start.38
  988.5 4.6 collective-permute-done.37
  993.1 6.8 collective-permute-done.38
  (415 shorter events, 128.7 us)
Async XLA Ops:
  0.7 29.9 %copy-start.59 = (bf16[96,768]{1,0:T(8,128)(2,1)S(1)}, bf16[96,768]{1,0:T(8,128)(2,1)}, u32[]{:S(2)}) copy-start(bf16[96,768]{1,0:T(8,128)(2,1)} %param.34) | copy-start | bytes 442372
  7.7 18.9 %collective-permute-start.1 = (bf16[4,24,768]{2,1,0:T(8,128)(2,1)S(1)}, bf16[4,24,768]{2,1,0:T(8,128)(2,1)S(1)}, u32[]{:S(2)}, u32[]{:S(2)}) collective-permute-start(bf16[4,24,768]{2,1,0:T(8,128)(2,1)S(1)} %get-tuple-element.127), channel_id=1, source_target_pairs={{0,4},{1,5},{2,6},{3,7},{4,0},{5,1},{6,2},{7,3},{8,12},{9,13},{10,... | collective-permute-start | bytes 442376 | tf_op jit(solution)/shard_map/ppermute | solution.py:58
  10.8 18.3 %collective-permute-start.2 = (bf16[4,24,768]{2,1,0:T(8,128)(2,1)S(1)}, bf16[4,24,768]{2,1,0:T(8,128)(2,1)S(1)}, u32[]{:S(2)}, u32[]{:S(2)}) collective-permute-start(bf16[4,24,768]{2,1,0:T(8,128)(2,1)S(1)} %get-tuple-element.127), channel_id=1, source_target_pairs={{0,8},{1,9},{2,10},{3,11},{4,12},{5,13},{6,14},{7,15},{8,0},{9,1},... | collective-permute-start | bytes 442376 | tf_op jit(solution)/shard_map/ppermute | solution.py:58
  13.4 17.2 %collective-permute-start.3 = (bf16[4,24,768]{2,1,0:T(8,128)(2,1)S(1)}, bf16[4,24,768]{2,1,0:T(8,128)(2,1)S(1)}, u32[]{:S(2)}, u32[]{:S(2)}) collective-permute-start(bf16[4,24,768]{2,1,0:T(8,128)(2,1)S(1)} %get-tuple-element.127), channel_id=1, source_target_pairs={{0,12},{1,13},{2,14},{3,15},{4,8},{5,9},{6,10},{7,11},{8,4},{9,5},... | collective-permute-start | bytes 442376 | tf_op jit(solution)/shard_map/ppermute | solution.py:58
  17.2 44.8 %collective-permute-start.10 = (bf16[6,24,768]{2,1,0:T(8,128)(2,1)S(1)}, bf16[6,24,768]{2,1,0:T(8,128)(2,1)S(1)}, u32[]{:S(2)}, u32[]{:S(2)}) collective-permute-start(bf16[6,24,768]{2,1,0:T(8,128)(2,1)S(1)} %constant_dynamic-update-slice_fusion), channel_id=1, source_target_pairs={{0,4},{1,5},{2,6},{3,7},{4,0},{5,1},{6,2},{7,3},{8,12},{9,13},{10,... | collective-permute-start | bytes 663560 | tf_op jit(solution)/shard_map/ppermute | solution.py:58
  18.1 15.0 %collective-permute-start.19 = (bf16[4,24,768]{2,1,0:T(8,128)(2,1)}, bf16[4,24,768]{2,1,0:T(8,128)(2,1)S(1)}, u32[]{:S(2)}, u32[]{:S(2)}) collective-permute-start(bf16[4,24,768]{2,1,0:T(8,128)(2,1)} %bitcast.391), channel_id=1, source_target_pairs={{0,4},{1,5},{2,6},{3,7},{4,0},{5,1},{6,2},{7,3},{8,12},{9,13},{10,... | collective-permute-start | bytes 442376 | tf_op jit(solution)/shard_map/ppermute | solution.py:58
  26.6 35.4 %collective-permute-start.11 = (bf16[6,24,768]{2,1,0:T(8,128)(2,1)S(1)}, bf16[6,24,768]{2,1,0:T(8,128)(2,1)S(1)}, u32[]{:S(2)}, u32[]{:S(2)}) collective-permute-start(bf16[6,24,768]{2,1,0:T(8,128)(2,1)S(1)} %constant_dynamic-update-slice_fusion), channel_id=1, source_target_pairs={{0,8},{1,9},{2,10},{3,11},{4,12},{5,13},{6,14},{7,15},{8,0},{9,1},... | collective-permute-start | bytes 663560 | tf_op jit(solution)/shard_map/ppermute | solution.py:58
  29.1 33.0 %collective-permute-start.12 = (bf16[6,24,768]{2,1,0:T(8,128)(2,1)S(1)}, bf16[6,24,768]{2,1,0:T(8,128)(2,1)S(1)}, u32[]{:S(2)}, u32[]{:S(2)}) collective-permute-start(bf16[6,24,768]{2,1,0:T(8,128)(2,1)S(1)} %constant_dynamic-update-slice_fusion), channel_id=1, source_target_pairs={{0,12},{1,13},{2,14},{3,15},{4,8},{5,9},{6,10},{7,11},{8,4},{9,5},... | collective-permute-start | bytes 663560 | tf_op jit(solution)/shard_map/ppermute | solution.py:58
  30.6 28.4 %collective-permute-start.20 = (bf16[4,24,768]{2,1,0:T(8,128)(2,1)S(1)}, bf16[4,24,768]{2,1,0:T(8,128)(2,1)S(1)}, u32[]{:S(2)}, u32[]{:S(2)}) collective-permute-start(bf16[4,24,768]{2,1,0:T(8,128)(2,1)S(1)} %bitcast.392), channel_id=1, source_target_pairs={{0,8},{1,9},{2,10},{3,11},{4,12},{5,13},{6,14},{7,15},{8,0},{9,1},... | collective-permute-start | bytes 442376 | tf_op jit(solution)/shard_map/ppermute | solution.py:58
  33.1 27.4 %collective-permute-start.21 = (bf16[4,24,768]{2,1,0:T(8,128)(2,1)S(1)}, bf16[4,24,768]{2,1,0:T(8,128)(2,1)S(1)}, u32[]{:S(2)}, u32[]{:S(2)}) collective-permute-start(bf16[4,24,768]{2,1,0:T(8,128)(2,1)S(1)} %bitcast.393), channel_id=1, source_target_pairs={{0,12},{1,13},{2,14},{3,15},{4,8},{5,9},{6,10},{7,11},{8,4},{9,5},... | collective-permute-start | bytes 442376 | tf_op jit(solution)/shard_map/ppermute | solution.py:58
  33.9 35.0 %copy-start.32 = (bf16[4,2,24,768]{3,2,1,0:T(8,128)(2,1)}, bf16[4,2,24,768]{3,2,1,0:T(8,128)(2,1)S(1)}, u32[]{:S(2)}) copy-start(bf16[4,2,24,768]{3,2,1,0:T(8,128)(2,1)S(1)} %get-tuple-element.106) | copy-start | bytes 884740
  34.0 40.6 %copy-start.30 = (bf16[4,2,24,768]{3,2,1,0:T(8,128)(2,1)}, bf16[4,2,24,768]{3,2,1,0:T(8,128)(2,1)S(1)}, u32[]{:S(2)}) copy-start(bf16[4,2,24,768]{3,2,1,0:T(8,128)(2,1)S(1)} %get-tuple-element.107) | copy-start | bytes 884740
  59.0 9.9 collective-permute-start.6
  60.5 13.5 %collective-permute-start.4 = (bf16[4,2,24,768]{3,2,1,0:T(8,128)(2,1)S(1)}, bf16[4,2,24,768]{3,2,1,0:T(8,128)(2,1)}, u32[]{:S(2)}, u32[]{:S(2)}) collective-permute-start(bf16[4,2,24,768]{3,2,1,0:T(8,128)(2,1)S(1)} %get-tuple-element.107), channel_id=1, source_target_pairs={{0,1},{1,0},{2,3},{3,2},{4,5},{5,4},{6,7},{7,6},{8,9},{9,8},{10,11... | collective-permute-start | bytes 884744 | tf_op jit(solution)/shard_map/ppermute | solution.py:58
  62.3 25.5 %copy-start.20 = (bf16[4,3,24,768]{3,2,1,0:T(8,128)(2,1)}, bf16[4,3,24,768]{3,2,1,0:T(8,128)(2,1)S(1)}, u32[]{:S(2)}) copy-start(bf16[4,3,24,768]{3,2,1,0:T(8,128)(2,1)S(1)} %get-tuple-element.96) | copy-start | bytes 1327108
  62.3 18.0 %collective-permute-start.15 = (bf16[4,3,24,768]{3,2,1,0:T(8,128)(2,1)S(1)}, bf16[4,3,24,768]{3,2,1,0:T(8,128)(2,1)}, u32[]{:S(2)}, u32[]{:S(2)}) collective-permute-start(bf16[4,3,24,768]{3,2,1,0:T(8,128)(2,1)S(1)} %get-tuple-element.96), channel_id=1, source_target_pairs={{0,2},{1,3},{2,0},{3,1},{4,6},{5,7},{6,4},{7,5},{8,10},{9,11},{10,... | collective-permute-start | bytes 1327112 | tf_op jit(solution)/shard_map/ppermute | solution.py:58
  62.9 24.8 %copy-start.29 = (bf16[4,2,24,768]{3,2,1,0:T(8,128)(2,1)}, bf16[4,2,24,768]{3,2,1,0:T(8,128)(2,1)S(1)}, u32[]{:S(2)}) copy-start(bf16[4,2,24,768]{3,2,1,0:T(8,128)(2,1)S(1)} %get-tuple-element.105) | copy-start | bytes 884740
  62.9 13.8 %collective-permute-start.22 = (bf16[4,2,24,768]{3,2,1,0:T(8,128)(2,1)S(1)}, bf16[4,2,24,768]{3,2,1,0:T(8,128)(2,1)S(1)}, u32[]{:S(2)}, u32[]{:S(2)}) collective-permute-start(bf16[4,2,24,768]{3,2,1,0:T(8,128)(2,1)S(1)} %get-tuple-element.105), channel_id=1, source_target_pairs={{0,1},{1,0},{2,3},{3,2},{4,5},{5,4},{6,7},{7,6},{8,9},{9,8},{10,11... | collective-permute-start | bytes 884744 | tf_op jit(solution)/shard_map/ppermute | solution.py:58
  63.5 16.7 %collective-permute-start.24 = (bf16[4,2,24,768]{3,2,1,0:T(8,128)(2,1)S(1)}, bf16[4,2,24,768]{3,2,1,0:T(8,128)(2,1)S(1)}, u32[]{:S(2)}, u32[]{:S(2)}) collective-permute-start(bf16[4,2,24,768]{3,2,1,0:T(8,128)(2,1)S(1)} %get-tuple-element.104), channel_id=1, source_target_pairs={{0,2},{1,3},{2,0},{3,1},{4,6},{5,7},{6,4},{7,5},{8,10},{9,11},{10,... | collective-permute-start | bytes 884744 | tf_op jit(solution)/shard_map/ppermute | solution.py:58
  69.6 16.7 %collective-permute-start.13 = (bf16[4,3,24,768]{3,2,1,0:T(8,128)(2,1)S(1)}, bf16[4,3,24,768]{3,2,1,0:T(8,128)(2,1)}, u32[]{:S(2)}, u32[]{:S(2)}) collective-permute-start(bf16[4,3,24,768]{3,2,1,0:T(8,128)(2,1)S(1)} %get-tuple-element.97), channel_id=1, source_target_pairs={{0,1},{1,0},{2,3},{3,2},{4,5},{5,4},{6,7},{7,6},{8,9},{9,8},{10,11... | collective-permute-start | bytes 1327112 | tf_op jit(solution)/shard_map/ppermute | solution.py:58
  74.0 21.9 %collective-permute-start.7 = (bf16[8,2,24,768]{3,2,1,0:T(8,128)(2,1)S(1)}, bf16[8,2,24,768]{3,2,1,0:T(8,128)(2,1)S(1)}, u32[]{:S(2)}, u32[]{:S(2)}) collective-permute-start(bf16[8,2,24,768]{3,2,1,0:T(8,128)(2,1)S(1)} %pad_maximum_fusion.33), channel_id=1, source_target_pairs={{0,1},{1,0},{2,3},{3,2},{4,5},{5,4},{6,7},{7,6},{8,9},{9,8},{10,11... | collective-permute-start | bytes 1769480 | tf_op jit(solution)/shard_map/ppermute | solution.py:58
  76.7 23.5 %collective-permute-start = (bf16[2,246,768]{2,1,0:T(8,128)(2,1)}, bf16[2,246,768]{2,1,0:T(8,128)(2,1)S(1)}, u32[]{:S(2)}, u32[]{:S(2)}) collective-permute-start(bf16[2,246,768]{2,1,0:T(8,128)(2,1)} %copy.127), channel_id=1, source_target_pairs={{0,16},{16,0},{1,17},{17,1},{2,18},{18,2},{3,19},{19,3},{4,20},{20... | collective-permute-start | bytes 2267144 | tf_op jit(solution)/shard_map/ppermute | solution.py:62
  80.2 21.2 %collective-permute-start.29 = (bf16[2,256,768]{2,1,0:T(8,128)(2,1)}, bf16[2,256,768]{2,1,0:T(8,128)(2,1)S(1)}, u32[]{:S(2)}, u32[]{:S(2)}) collective-permute-start(bf16[2,256,768]{2,1,0:T(8,128)(2,1)} %constant_dynamic-slice_fusion.6), channel_id=1, source_target_pairs={{0,16},{16,0},{1,17},{17,1},{2,18},{18,2},{3,19},{19,3},{4,20},{20... | collective-permute-start | bytes 2359304 | tf_op jit(solution)/shard_map/ppermute | solution.py:62
  80.2 17.3 %collective-permute-start.5 = (bf16[8,2,24,768]{3,2,1,0:T(8,128)(2,1)S(1)}, bf16[8,2,24,768]{3,2,1,0:T(8,128)(2,1)S(1)}, u32[]{:S(2)}, u32[]{:S(2)}) collective-permute-start(bf16[8,2,24,768]{3,2,1,0:T(8,128)(2,1)S(1)} %pad_maximum_fusion.32), channel_id=1, source_target_pairs={{0,2},{1,3},{2,0},{3,1},{4,6},{5,7},{6,4},{7,5},{8,10},{9,11},{10,... | collective-permute-start | bytes 1769480 | tf_op jit(solution)/shard_map/ppermute | solution.py:58
  86.3 22.8 %collective-permute-start.23 = (bf16[8,2,24,768]{3,2,1,0:T(8,128)(2,1)S(1)}, bf16[8,2,24,768]{3,2,1,0:T(8,128)(2,1)S(1)}, u32[]{:S(2)}, u32[]{:S(2)}) collective-permute-start(bf16[8,2,24,768]{3,2,1,0:T(8,128)(2,1)S(1)} %pad_maximum_fusion.35), channel_id=1, source_target_pairs={{0,2},{1,3},{2,0},{3,1},{4,6},{5,7},{6,4},{7,5},{8,10},{9,11},{10,... | collective-permute-start | bytes 1769480 | tf_op jit(solution)/shard_map/ppermute | solution.py:58
  95.9 19.0 %collective-permute-start.25 = (bf16[8,2,24,768]{3,2,1,0:T(8,128)(2,1)}, bf16[8,2,24,768]{3,2,1,0:T(8,128)(2,1)}, u32[]{:S(2)}, u32[]{:S(2)}) collective-permute-start(bf16[8,2,24,768]{3,2,1,0:T(8,128)(2,1)} %pad_maximum_fusion.36), channel_id=1, source_target_pairs={{0,1},{1,0},{2,3},{3,2},{4,5},{5,4},{6,7},{7,6},{8,9},{9,8},{10,11... | collective-permute-start | bytes 1769480 | tf_op jit(solution)/shard_map/ppermute | solution.py:58
  97.5 28.2 %collective-permute-start.16 = (bf16[8,3,24,768]{3,2,1,0:T(8,128)(2,1)}, bf16[8,3,24,768]{3,2,1,0:T(8,128)(2,1)}, u32[]{:S(2)}, u32[]{:S(2)}) collective-permute-start(bf16[8,3,24,768]{3,2,1,0:T(8,128)(2,1)} %pad_maximum_fusion.28), channel_id=1, source_target_pairs={{0,1},{1,0},{2,3},{3,2},{4,5},{5,4},{6,7},{7,6},{8,9},{9,8},{10,11... | collective-permute-start | bytes 2654216 | tf_op jit(solution)/shard_map/ppermute | solution.py:58
  100.2 28.2 %collective-permute-start.14 = (bf16[8,3,24,768]{3,2,1,0:T(8,128)(2,1)}, bf16[8,3,24,768]{3,2,1,0:T(8,128)(2,1)}, u32[]{:S(2)}, u32[]{:S(2)}) collective-permute-start(bf16[8,3,24,768]{3,2,1,0:T(8,128)(2,1)} %pad_maximum_fusion.27), channel_id=1, source_target_pairs={{0,2},{1,3},{2,0},{3,1},{4,6},{5,7},{6,4},{7,5},{8,10},{9,11},{10,... | collective-permute-start | bytes 2654216 | tf_op jit(solution)/shard_map/ppermute | solution.py:58
  101.4 30.2 %collective-permute-start.9 = (bf16[16,2,24,768]{3,2,1,0:T(8,128)(2,1)S(1)}, bf16[16,2,24,768]{3,2,1,0:T(8,128)(2,1)}, u32[]{:S(2)}, u32[]{:S(2)}) collective-permute-start(bf16[16,2,24,768]{3,2,1,0:T(8,128)(2,1)S(1)} %pad_maximum_fusion.13.b_ref), channel_id=1, source_target_pairs={{0,16},{16,0},{1,17},{17,1},{2,18},{18,2},{3,19},{19,3},{4,20},{20... | collective-permute-start | bytes 3538952 | tf_op jit(solution)/shard_map/ppermute | solution.py:62
  109.1 22.5 %collective-permute-start.8 = (bf16[16,2,24,768]{3,2,1,0:T(8,128)(2,1)}, bf16[16,2,24,768]{3,2,1,0:T(8,128)(2,1)}, u32[]{:S(2)}, u32[]{:S(2)}) collective-permute-start(bf16[16,2,24,768]{3,2,1,0:T(8,128)(2,1)} %pad_maximum_fusion.12.a_ref), channel_id=1, source_target_pairs={{0,16},{16,0},{1,17},{17,1},{2,18},{18,2},{3,19},{19,3},{4,20},{20... | collective-permute-start | bytes 3538952 | tf_op jit(solution)/shard_map/ppermute | solution.py:62
  114.9 198.0 %collective-permute-start.26 = (bf16[16,2,24,768]{3,2,1,0:T(8,128)(2,1)}, bf16[16,2,24,768]{3,2,1,0:T(8,128)(2,1)}, u32[]{:S(2)}, u32[]{:S(2)}) collective-permute-start(bf16[16,2,24,768]{3,2,1,0:T(8,128)(2,1)} %pad_maximum_fusion.14.a_ref), channel_id=1, source_target_pairs={{0,16},{16,0},{1,17},{17,1},{2,18},{18,2},{3,19},{19,3},{4,20},{20... | collective-permute-start | bytes 3538952 | tf_op jit(solution)/shard_map/ppermute | solution.py:62
  125.7 187.2 %collective-permute-start.27 = (bf16[16,2,24,768]{3,2,1,0:T(8,128)(2,1)}, bf16[16,2,24,768]{3,2,1,0:T(8,128)(2,1)}, u32[]{:S(2)}, u32[]{:S(2)}) collective-permute-start(bf16[16,2,24,768]{3,2,1,0:T(8,128)(2,1)} %pad_maximum_fusion.15.b_ref), channel_id=1, source_target_pairs={{0,16},{16,0},{1,17},{17,1},{2,18},{18,2},{3,19},{19,3},{4,20},{20... | collective-permute-start | bytes 3538952 | tf_op jit(solution)/shard_map/ppermute | solution.py:62
  128.4 336.9 %collective-permute-start.18 = (bf16[16,3,24,768]{3,2,1,0:T(8,128)(2,1)}, bf16[16,3,24,768]{3,2,1,0:T(8,128)(2,1)}, u32[]{:S(2)}, u32[]{:S(2)}) collective-permute-start(bf16[16,3,24,768]{3,2,1,0:T(8,128)(2,1)} %pad_maximum_fusion.3.b_ref), channel_id=1, source_target_pairs={{0,16},{16,0},{1,17},{17,1},{2,18},{18,2},{3,19},{19,3},{4,20},{20... | collective-permute-start | bytes 5308424 | tf_op jit(solution)/shard_map/ppermute | solution.py:62
  131.6 333.7 %collective-permute-start.17 = (bf16[16,3,24,768]{3,2,1,0:T(8,128)(2,1)}, bf16[16,3,24,768]{3,2,1,0:T(8,128)(2,1)}, u32[]{:S(2)}, u32[]{:S(2)}) collective-permute-start(bf16[16,3,24,768]{3,2,1,0:T(8,128)(2,1)} %pad_maximum_fusion.2.a_ref), channel_id=1, source_target_pairs={{0,16},{16,0},{1,17},{17,1},{2,18},{18,2},{3,19},{19,3},{4,20},{20... | collective-permute-start | bytes 5308424 | tf_op jit(solution)/shard_map/ppermute | solution.py:62
  312.9 144.7 %copy-start.22 = (bf16[512,768]{0,1:T(8,128)(2,1)S(1)}, bf16[512,768]{0,1:T(8,128)(2,1)}, u32[]{:S(2)}) copy-start(bf16[512,768]{0,1:T(8,128)(2,1)} %get-tuple-element.86) | copy-start | bytes 2359300
  686.3 52.9 %slice-start.12 = ((s8[4718592]{0:T(1024)(128)(4,1)}), s8[4194304]{0:T(1024)(128)(4,1)S(1)}, s32[]{:S(2)}) async-start(s8[4718592]{0:T(1024)(128)(4,1)} %bitcast.334), calls=%async_computation.12 | async-start | bytes 8388608
  689.6 49.6 %slice-start.13 = ((s8[4718592]{0:T(1024)(128)(4,1)}), s8[524288]{0:T(1024)(128)(4,1)S(1)}, s32[]{:S(2)}) async-start(s8[4718592]{0:T(1024)(128)(4,1)} %bitcast.334), calls=%async_computation.13 | async-start | bytes 1048576
  863.9 26.9 %collective-permute-start.48 = (bf16[4,2,2,4,24,768]{5,4,3,2,1,0:T(8,128)(2,1)}, bf16[4,2,2,4,24,768]{5,4,3,2,1,0:T(8,128)(2,1)}, u32[]{:S(2)}, u32[]{:S(2)}) collective-permute-start(bf16[4,2,2,4,24,768]{5,4,3,2,1,0:T(8,128)(2,1)} %dynamic-slice_bitcast_fusion.1), channel_id=1, source_target_pairs={{0,16},{16,0},{1,17},{17,1},{2,18},{18,2},{3,19},{19,3},{4,20},{20... | collective-permute-start | bytes 7077896 | tf_op jit(solution)/shard_map/ppermute | solution.py:62
  869.1 26.0 %collective-permute-start.40 = (bf16[4,2,2,4,24,768]{5,4,3,0,1,2:T(8,128)(2,1)}, bf16[4,2,2,4,24,768]{5,4,3,0,1,2:T(8,128)(2,1)}, u32[]{:S(2)}, u32[]{:S(2)}) collective-permute-start(bf16[4,2,2,4,24,768]{5,4,3,0,1,2:T(8,128)(2,1)} %bitcast.297), channel_id=1, source_target_pairs={{0,16},{16,0},{1,17},{17,1},{2,18},{18,2},{3,19},{19,3},{4,20},{20... | collective-permute-start | bytes 7077896 | tf_op jit(solution)/shard_map/ppermute | solution.py:62
  877.6 9.7 collective-permute-start.30
  879.6 70.1 %collective-permute-start.32 = (bf16[4,2,2,6,24,768]{5,4,2,1,0,3:T(8,128)(2,1)S(1)}, bf16[4,2,2,6,24,768]{5,4,2,1,0,3:T(8,128)(2,1)S(1)}, u32[]{:S(2)}, u32[]{:S(2)}) collective-permute-start(bf16[4,2,2,6,24,768]{5,4,2,1,0,3:T(8,128)(2,1)S(1)} %dynamic-slice_bitcast_fusion), channel_id=1, source_target_pairs={{0,16},{16,0},{1,17},{17,1},{2,18},{18,2},{3,19},{19,3},{4,20},{20... | collective-permute-start | bytes 10616840 | tf_op jit(solution)/shard_map/ppermute | solution.py:62
  880.1 6.0 collective-permute-start.31
  886.1 3.3 collective-permute-start.28
  893.5 16.2 %collective-permute-start.51 = (bf16[4,2,2,24,768]{4,3,2,1,0:T(8,128)(2,1)S(1)}, bf16[4,2,2,24,768]{4,3,2,1,0:T(8,128)(2,1)S(1)}, u32[]{:S(2)}, u32[]{:S(2)}) collective-permute-start(bf16[4,2,2,24,768]{4,3,2,1,0:T(8,128)(2,1)S(1)} %dynamic-slice_bitcast_fusion.3), channel_id=1, source_target_pairs={{0,1},{1,0},{2,3},{3,2},{4,5},{5,4},{6,7},{7,6},{8,9},{9,8},{10,11... | collective-permute-start | bytes 1769480 | tf_op jit(solution)/shard_map/ppermute | solution.py:58
  897.7 23.9 %collective-permute-start.43 = (bf16[4,2,2,24,768]{4,3,2,0,1:T(8,128)(2,1)S(1)}, bf16[4,2,2,24,768]{4,3,2,0,1:T(8,128)(2,1)S(1)}, u32[]{:S(2)}, u32[]{:S(2)}) collective-permute-start(bf16[4,2,2,24,768]{4,3,2,0,1:T(8,128)(2,1)S(1)} %dynamic-slice_bitcast_fusion.4), channel_id=1, source_target_pairs={{0,1},{1,0},{2,3},{3,2},{4,5},{5,4},{6,7},{7,6},{8,9},{9,8},{10,11... | collective-permute-start | bytes 1769480 | tf_op jit(solution)/shard_map/ppermute | solution.py:58
  899.2 30.0 %collective-permute-start.49 = (bf16[4,2,2,24,768]{4,3,2,0,1:T(8,128)(2,1)S(1)}, bf16[4,2,2,24,768]{4,3,2,0,1:T(8,128)(2,1)S(1)}, u32[]{:S(2)}, u32[]{:S(2)}) collective-permute-start(bf16[4,2,2,24,768]{4,3,2,0,1:T(8,128)(2,1)S(1)} %bitcast.383), channel_id=1, source_target_pairs={{0,2},{1,3},{2,0},{3,1},{4,6},{5,7},{6,4},{7,5},{8,10},{9,11},{10,... | collective-permute-start | bytes 1769480 | tf_op jit(solution)/shard_map/ppermute | solution.py:58
  899.8 28.3 %collective-permute-start.41 = (bf16[4,2,2,24,768]{4,3,2,0,1:T(8,128)(2,1)S(1)}, bf16[4,2,2,24,768]{4,3,2,0,1:T(8,128)(2,1)S(1)}, u32[]{:S(2)}, u32[]{:S(2)}) collective-permute-start(bf16[4,2,2,24,768]{4,3,2,0,1:T(8,128)(2,1)S(1)} %dynamic-slice_bitcast_fusion.5), channel_id=1, source_target_pairs={{0,2},{1,3},{2,0},{3,1},{4,6},{5,7},{6,4},{7,5},{8,10},{9,11},{10,... | collective-permute-start | bytes 1769480 | tf_op jit(solution)/shard_map/ppermute | solution.py:58
  910.0 38.2 %collective-permute-start.52 = (bf16[4,2,24,768]{3,2,1,0:T(8,128)(2,1)S(1)}, bf16[4,2,24,768]{3,2,1,0:T(8,128)(2,1)S(1)}, u32[]{:S(2)}, u32[]{:S(2)}) collective-permute-start(bf16[4,2,24,768]{3,2,1,0:T(8,128)(2,1)S(1)} %dynamic-slice_bitcast_fusion.8), channel_id=1, source_target_pairs={{0,2},{1,3},{2,0},{3,1},{4,6},{5,7},{6,4},{7,5},{8,10},{9,11},{10,... | collective-permute-start | bytes 884744 | tf_op jit(solution)/shard_map/ppermute | solution.py:58
  921.8 17.8 %collective-permute-start.44 = (bf16[4,2,24,768]{3,2,1,0:T(8,128)(2,1)S(1)}, bf16[4,2,24,768]{3,2,1,0:T(8,128)(2,1)S(1)}, u32[]{:S(2)}, u32[]{:S(2)}) collective-permute-start(bf16[4,2,24,768]{3,2,1,0:T(8,128)(2,1)S(1)} %dynamic-slice_bitcast_fusion.10), channel_id=1, source_target_pairs={{0,2},{1,3},{2,0},{3,1},{4,6},{5,7},{6,4},{7,5},{8,10},{9,11},{10,... | collective-permute-start | bytes 884744 | tf_op jit(solution)/shard_map/ppermute | solution.py:58
  928.3 11.4 %collective-permute-start.42 = (bf16[4,2,24,768]{3,2,1,0:T(8,128)(2,1)S(1)}, bf16[4,2,24,768]{3,2,1,0:T(8,128)(2,1)S(1)}, u32[]{:S(2)}, u32[]{:S(2)}) collective-permute-start(bf16[4,2,24,768]{3,2,1,0:T(8,128)(2,1)S(1)} %dynamic-slice_bitcast_fusion.11), channel_id=1, source_target_pairs={{0,1},{1,0},{2,3},{3,2},{4,5},{5,4},{6,7},{7,6},{8,9},{9,8},{10,11... | collective-permute-start | bytes 884744 | tf_op jit(solution)/shard_map/ppermute | solution.py:58
  929.3 22.8 %collective-permute-start.50 = (bf16[4,2,24,768]{3,2,1,0:T(8,128)(2,1)S(1)}, bf16[4,2,24,768]{3,2,1,0:T(8,128)(2,1)S(1)}, u32[]{:S(2)}, u32[]{:S(2)}) collective-permute-start(bf16[4,2,24,768]{3,2,1,0:T(8,128)(2,1)S(1)} %dynamic-slice_bitcast_fusion.9), channel_id=1, source_target_pairs={{0,1},{1,0},{2,3},{3,2},{4,5},{5,4},{6,7},{7,6},{8,9},{9,8},{10,11... | collective-permute-start | bytes 884744 | tf_op jit(solution)/shard_map/ppermute | solution.py:58
  939.9 14.2 %collective-permute-start.45 = (bf16[4,24,768]{2,1,0:T(8,128)(2,1)S(1)}, bf16[4,24,768]{2,1,0:T(8,128)(2,1)S(1)}, u32[]{:S(2)}, u32[]{:S(2)}) collective-permute-start(bf16[4,24,768]{2,1,0:T(8,128)(2,1)S(1)} %get-tuple-element.101), channel_id=1, source_target_pairs={{0,4},{1,5},{2,6},{3,7},{4,0},{5,1},{6,2},{7,3},{8,12},{9,13},{10,... | collective-permute-start | bytes 442376 | tf_op jit(solution)/shard_map/ppermute | solution.py:58
  946.2 13.4 %collective-permute-start.46 = (bf16[4,24,768]{2,1,0:T(8,128)(2,1)S(1)}, bf16[4,24,768]{2,1,0:T(8,128)(2,1)S(1)}, u32[]{:S(2)}, u32[]{:S(2)}) collective-permute-start(bf16[4,24,768]{2,1,0:T(8,128)(2,1)S(1)} %get-tuple-element.102), channel_id=1, source_target_pairs={{0,8},{1,9},{2,10},{3,11},{4,12},{5,13},{6,14},{7,15},{8,0},{9,1},... | collective-permute-start | bytes 442376 | tf_op jit(solution)/shard_map/ppermute | solution.py:58
  948.2 12.3 %collective-permute-start.47 = (bf16[4,24,768]{2,1,0:T(8,128)(2,1)S(1)}, bf16[4,24,768]{2,1,0:T(8,128)(2,1)S(1)}, u32[]{:S(2)}, u32[]{:S(2)}) collective-permute-start(bf16[4,24,768]{2,1,0:T(8,128)(2,1)S(1)} %get-tuple-element.103), channel_id=1, source_target_pairs={{0,12},{1,13},{2,14},{3,15},{4,8},{5,9},{6,10},{7,11},{8,4},{9,5},... | collective-permute-start | bytes 442376 | tf_op jit(solution)/shard_map/ppermute | solution.py:58
  951.5 20.1 %collective-permute-start.35 = (bf16[4,2,3,24,768]{4,3,1,0,2:T(8,128)(2,1)S(1)}, bf16[4,2,3,24,768]{4,3,1,0,2:T(8,128)(2,1)S(1)}, u32[]{:S(2)}, u32[]{:S(2)}) collective-permute-start(bf16[4,2,3,24,768]{4,3,1,0,2:T(8,128)(2,1)S(1)} %dynamic-slice_bitcast_fusion.2), channel_id=1, source_target_pairs={{0,1},{1,0},{2,3},{3,2},{4,5},{5,4},{6,7},{7,6},{8,9},{9,8},{10,11... | collective-permute-start | bytes 2654216 | tf_op jit(solution)/shard_map/ppermute | solution.py:58
  952.4 21.0 %collective-permute-start.33 = (bf16[4,2,3,24,768]{4,3,0,2,1:T(8,128)(2,1)S(1)}, bf16[4,2,3,24,768]{4,3,0,2,1:T(8,128)(2,1)S(1)}, u32[]{:S(2)}, u32[]{:S(2)}) collective-permute-start(bf16[4,2,3,24,768]{4,3,0,2,1:T(8,128)(2,1)S(1)} %bitcast.378), channel_id=1, source_target_pairs={{0,2},{1,3},{2,0},{3,1},{4,6},{5,7},{6,4},{7,5},{8,10},{9,11},{10,... | collective-permute-start | bytes 2654216 | tf_op jit(solution)/shard_map/ppermute | solution.py:58
  954.0 32.3 %collective-permute-start.53 = (bf16[4,24,768]{2,1,0:T(8,128)(2,1)S(1)}, bf16[4,24,768]{2,1,0:T(8,128)(2,1)S(1)}, u32[]{:S(2)}, u32[]{:S(2)}) collective-permute-start(bf16[4,24,768]{2,1,0:T(8,128)(2,1)S(1)} %get-tuple-element.98), channel_id=1, source_target_pairs={{0,4},{1,5},{2,6},{3,7},{4,0},{5,1},{6,2},{7,3},{8,12},{9,13},{10,... | collective-permute-start | bytes 442376 | tf_op jit(solution)/shard_map/ppermute | solution.py:58
  959.7 28.1 %collective-permute-start.54 = (bf16[4,24,768]{2,1,0:T(8,128)(2,1)S(1)}, bf16[4,24,768]{2,1,0:T(8,128)(2,1)S(1)}, u32[]{:S(2)}, u32[]{:S(2)}) collective-permute-start(bf16[4,24,768]{2,1,0:T(8,128)(2,1)S(1)} %get-tuple-element.99), channel_id=1, source_target_pairs={{0,8},{1,9},{2,10},{3,11},{4,12},{5,13},{6,14},{7,15},{8,0},{9,1},... | collective-permute-start | bytes 442376 | tf_op jit(solution)/shard_map/ppermute | solution.py:58
  960.5 27.2 %collective-permute-start.55 = (bf16[4,24,768]{2,1,0:T(8,128)(2,1)S(1)}, bf16[4,24,768]{2,1,0:T(8,128)(2,1)S(1)}, u32[]{:S(2)}, u32[]{:S(2)}) collective-permute-start(bf16[4,24,768]{2,1,0:T(8,128)(2,1)S(1)} %get-tuple-element.100), channel_id=1, source_target_pairs={{0,12},{1,13},{2,14},{3,15},{4,8},{5,9},{6,10},{7,11},{8,4},{9,5},... | collective-permute-start | bytes 442376 | tf_op jit(solution)/shard_map/ppermute | solution.py:58
  971.8 9.6 collective-permute-start.36
  973.7 9.4 collective-permute-start.34
  983.3 9.8 collective-permute-start.37
  983.9 16.0 %collective-permute-start.38 = (bf16[6,24,768]{2,1,0:T(8,128)(2,1)S(1)}, bf16[6,24,768]{2,1,0:T(8,128)(2,1)S(1)}, u32[]{:S(2)}, u32[]{:S(2)}) collective-permute-start(bf16[6,24,768]{2,1,0:T(8,128)(2,1)S(1)} %get-tuple-element.94), channel_id=1, source_target_pairs={{0,8},{1,9},{2,10},{3,11},{4,12},{5,13},{6,14},{7,15},{8,0},{9,1},... | collective-permute-start | bytes 663560 | tf_op jit(solution)/shard_map/ppermute | solution.py:58
  986.3 13.6 %collective-permute-start.39 = (bf16[6,24,768]{2,1,0:T(8,128)(2,1)S(1)}, bf16[6,24,768]{2,1,0:T(8,128)(2,1)S(1)}, u32[]{:S(2)}, u32[]{:S(2)}) collective-permute-start(bf16[6,24,768]{2,1,0:T(8,128)(2,1)S(1)} %get-tuple-element.95), channel_id=1, source_target_pairs={{0,12},{1,13},{2,14},{3,15},{4,8},{5,9},{6,10},{7,11},{8,4},{9,5},... | collective-permute-start | bytes 663560 | tf_op jit(solution)/shard_map/ppermute | solution.py:58
  (74 other events, 457.0 us)
